TPU v7x, 128 devices: a whole 4x4x4 slice. The times are simulated.
128 devices in a mesh: expert: 64 (over z, x, y_lo, core), dp: 2 (over y_hi).
Axes of the slice: x: 4, y: 4 (y_hi: 2, y_lo: 2; y = y_hi * 2 + y_lo), z: 4, core: 2. Of those that a mesh axis runs over, the one named last changes fastest.
Arguments:
- tokens: bfloat16 [2, 32768, 1024], P('dp', 'expert'), may hold values from -6 to 6
- cotangent: bfloat16 [2, 32768, 1024], P('dp', 'expert'), may hold values from -6 to 6
- assign: int32 [2, 32768], P('dp', 'expert'), may hold values from 0 to 32767, as said below
- gain: float32 [64, 1024], P('expert'), may hold values from 0.1 to 1.9
- router: bfloat16 [64, 1024], P('expert'), may hold values from -0.1875 to 0.1875
- w_in: bfloat16 [64, 2048, 1024], P('expert', 'dp'), may hold values from -0.1875 to 0.1875
- w_out: bfloat16 [64, 2048, 1024], P('expert', 'dp'), may hold values from -0.125 to 0.125
Outputs:
- mixed: bfloat16 [2, 32768, 1024], P('dp', 'expert')
- input_grad: bfloat16 [2, 32768, 1024], P('dp', 'expert')
- w_in_grad: float32 [64, 2048, 1024], P('expert', 'dp')
- w_out_grad: float32 [64, 2048, 1024], P('expert', 'dp')
- gain_grad: float32 [64, 1024], P('expert')
- router_grad: float32 [64, 1024], P('expert')
Inputs may be any that keep to these rules, and one draw needn't show every extreme that they name: Each row of assign is a permutation of the 32768 slots, so every expert receives 512 tokens of each group. Of the 512 tokens of one device, at most 16 go to one expert, and in every draw each device sends exactly 16 to some expert.
All inputs are finite; a program needn't handle non-finite values.
Results may differ from a plain program's by a relative error of at most 0.0062.
Values may be sent and summed in bfloat16 or wider, within the bound.
No kernel may reach another device: no remote copies, remote signals or barrier semaphores. Data moves between devices by JAX's collectives and lax.ppermute only.
A program may use at most 192 MiB of HBM per device.

v0:
```python
import jax
import jax.numpy as jnp
from jax import lax
from jax.sharding import PartitionSpec as P

EPS = 1e-05


def gelu_fn(values):
    return jax.nn.gelu(values, approximate=True)


def normalize(rows, gain_row):
    xf = rows.astype(jnp.float32)
    inv = lax.rsqrt(jnp.mean(xf * xf, -1, keepdims=True) + EPS)
    unit = xf * inv
    return (inv, unit, (unit * gain_row).astype(jnp.bfloat16))


def gate_of(rows, router_row):
    return jax.nn.sigmoid(jnp.dot(rows, router_row, preferred_element_type=jnp.float32))[:, None]


def transposed_product(left, right):
    return lax.dot_general(
        left, right, (((0,), (0,)), ((), ())), preferred_element_type=jnp.float32
    )


def local(tokens, cotangent, assign, gain, router, w_in, w_out):
    experts = lax.axis_size("expert")
    tok = tokens.shape[1]
    width = tokens.shape[2]
    cap = 2 * tok // experts
    slots_all = experts * cap
    target = assign[0] // tok
    onehot = (target[:, None] == jnp.arange(experts, dtype=jnp.int32)[None, :]).astype(jnp.int32)
    rank = jnp.sum((jnp.cumsum(onehot, 0) - onehot) * onehot, 1)
    where = target * cap + rank

    def pack(rows):
        return (
            jnp.zeros((slots_all, width), rows.dtype)
            .at[where]
            .set(rows)
            .reshape(experts, cap, width)
        )

    def unpack(buffer):
        return buffer.reshape(slots_all, width)[where]

    gain_row = gain[0]
    router_row = router[0]
    w_in_own = w_in[0]
    w_out_own = w_out[0]
    x_buf = lax.all_to_all(pack(tokens[0]), "expert", split_axis=0, concat_axis=0, tiled=True)
    x_rows = x_buf.reshape(slots_all, width)
    full_in, full_out = (
        lax.all_gather(w_in_own, "dp", axis=0, tiled=True),
        lax.all_gather(w_out_own, "dp", axis=0, tiled=True),
    )
    inv_all, unit_all, normed = normalize(x_rows, gain_row)
    pre = jnp.dot(normed, full_in.T, preferred_element_type=jnp.float32)
    hid = gelu_fn(pre).astype(jnp.bfloat16)
    branch = jnp.dot(hid, full_out, preferred_element_type=jnp.float32)
    gate = gate_of(x_rows, router_row)
    xf = x_rows.astype(jnp.float32)
    y_rows = (xf + gate * branch).astype(jnp.bfloat16)
    mixed = unpack(
        lax.all_to_all(
            y_rows.reshape(experts, cap, width), "expert", split_axis=0, concat_axis=0, tiled=True
        )
    )
    dy_rows = lax.all_to_all(
        pack(cotangent[0]), "expert", split_axis=0, concat_axis=0, tiled=True
    ).reshape(slots_all, width)
    dyf = dy_rows.astype(jnp.float32)
    dlogit = jnp.sum(dyf * branch, -1, keepdims=True) * gate * (1.0 - gate)
    pull = jax.vjp(gelu_fn, pre)[1]
    dbranch = (gate * dyf).astype(jnp.bfloat16)
    dhid = jnp.dot(dbranch, full_out.T, preferred_element_type=jnp.float32)
    dpre = pull(dhid)[0].astype(jnp.bfloat16)
    dnormed = jnp.dot(dpre, full_in, preferred_element_type=jnp.float32)
    grad_in = lax.psum_scatter(
        transposed_product(dpre, normed), "dp", scatter_dimension=0, tiled=True
    )
    grad_out = lax.psum_scatter(
        transposed_product(hid, dbranch), "dp", scatter_dimension=0, tiled=True
    )
    dunit = dnormed * gain_row
    back = (
        dyf
        + inv_all * (dunit - unit_all * jnp.mean(dunit * unit_all, -1, keepdims=True))
        + dlogit * router_row.astype(jnp.float32)
    )
    back_rows = back.astype(jnp.bfloat16)
    gain_part = jnp.sum(dnormed * unit_all, 0)
    router_part = jnp.sum(dlogit * xf, 0)
    gain_grad, router_grad = lax.psum((gain_part, router_part), "dp")
    input_grad = unpack(
        lax.all_to_all(
            back_rows.reshape(experts, cap, width),
            "expert",
            split_axis=0,
            concat_axis=0,
            tiled=True,
        )
    )
    return (
        mixed[None],
        input_grad[None],
        grad_in[None],
        grad_out[None],
        gain_grad[None],
        router_grad[None],
    )


def solution(mesh):
    return jax.shard_map(
        local,
        mesh=mesh,
        in_specs=(
            P("dp", "expert", None),
            P("dp", "expert", None),
            P("dp", "expert"),
            P("expert", None),
            P("expert", None),
            P("expert", "dp", None),
            P("expert", "dp", None),
        ),
        out_specs=(
            P("dp", "expert", None),
            P("dp", "expert", None),
            P("expert", "dp", None),
            P("expert", "dp", None),
            P("expert", None),
            P("expert", None),
        ),
        check_vma=False,
    )
```

profile of v0, /device:TPU:1, one launch (start us, length us, event | category | flops | bytes accessed | tf_op | source)
XLA Modules:
  0.0 476.9 jit_solution(12784455155844901778)
XLA Ops:
  7.2 0.0 copy-start
  7.2 0.0 copy-start.3
  7.2 0.0 all-gather.5.cloned.1.call-start
  7.2 0.7 all-gather.5.cloned.1.call-update
  7.9 0.0 all-gather.7.cloned.1.call-start
  8.0 0.7 all-gather.7.cloned.1.call-update
  8.7 0.0 copy-start.2
  8.7 0.0 copy-done.3
  8.7 1.2 reduce-window.6
  10.0 0.2 slice_reduce_fusion
  10.2 0.1 fusion.44
  10.4 0.0 copy-done
  10.4 4.1 scatter_custom_fusion
  14.5 10.8 %all-to-all-start = ((bf16[64,16,1024]{2,1,0:T(8,128)(2,1)}), bf16[64,16,1024]{2,1,0:T(8,128)(2,1)S(1)}, u32[]{:S(2)}, u32[]{:S(2)}) async-start(bf16[64,16,1024]{2,1,0:T(8,128)(2,1)} %bitcast.92), calls=%async_computation | async-start | bytes 4194304 | tf_op jit(solution)/shard_map/all_to_all | solution.py:56
  25.4 0.0 copy-done.2
  25.4 0.0 copy-start.4
  25.4 4.1 scatter_custom_fusion.1
  29.5 28.6 %all-to-all-done = bf16[64,16,1024]{2,1,0:T(8,128)(2,1)S(1)} async-done(((bf16[64,16,1024]{2,1,0:T(8,128)(2,1)}), bf16[64,16,1024]{2,1,0:T(8,128)(2,1)S(1)}, u32[]{:S(2)}, u32[]{:S(2)}) %all-to-all-start) | async-done | bytes 2097184 | tf_op jit(solution)/shard_map/all_to_all | solution.py:56
  58.1 0.0 copy-start.5
  58.1 6.8 %all-to-all-start.2 = ((bf16[64,16,1024]{2,1,0:T(8,128)(2,1)}), bf16[64,16,1024]{2,1,0:T(8,128)(2,1)}, u32[]{:S(2)}, u32[]{:S(2)}) async-start(bf16[64,16,1024]{2,1,0:T(8,128)(2,1)} %bitcast.91), calls=%async_computation.2 | async-start | bytes 4194304 | tf_op jit(solution)/shard_map/all_to_all | solution.py:74
  64.9 0.2 reduce-scatter.3.cloned.1.call-start
  65.2 0.5 fusion.17
  65.7 0.1 rsqrt.12
  65.7 0.0 copy-done.4
  65.7 0.6 fusion.46
  66.4 52.4 %all-gather.5.cloned.1.call-done = bf16[1,2048,1024]{2,1,0:T(8,128)(2,1)} async-done(((bf16[1,1024,1024]{2,1,0:T(8,128)(2,1)}), bf16[1,2048,1024]{2,1,0:T(8,128)(2,1)}) %all-gather.5.cloned.1.call-update) | async-done | bytes 4194320 | tf_op jit(solution)/shard_map/all_gather | solution.py:59
  118.8 0.0 copy-done.5
  118.8 9.1 %fusion.29 = f32[1024,2048]{1,0:T(8,128)} fusion(bf16[1,2048,1024]{2,1,0:T(8,128)(2,1)} %all-gather.5.cloned.1.call-done, bf16[1024,1024]{1,0:T(8,128)(2,1)S(1)} %bitcast.88, f32[1024]{0:T(1024)S(1)} %bitcast.105, f32[1024]{0:T(1024)S(1)} %rsqrt.12), kind=kOutput, calls=%fused_computation.43 | convolution fusion | flops 4299161600 | bytes 14688256 | tf_op jit(solution)/shard_map/dot_general | solution.py:63
  127.9 0.0 all-to-all-done.2
  127.9 55.8 %all-gather.7.cloned.1.call-done = bf16[1,2048,1024]{2,1,0:T(8,128)(2,1)} async-done(((bf16[1,1024,1024]{2,1,0:T(8,128)(2,1)}), bf16[1,2048,1024]{2,1,0:T(8,128)(2,1)}) %all-gather.7.cloned.1.call-update) | async-done | bytes 4194320 | tf_op jit(solution)/shard_map/all_gather | solution.py:60
  183.7 0.0 copy-start.6
  183.7 0.0 copy-start.7
  183.7 11.0 %fusion.22 = (f32[1024]{0:T(1024)S(1)}, bf16[1024,1024]{1,0:T(8,128)(2,1)}, bf16[1024,1024]{1,0:T(8,128)(2,1)S(1)}) fusion(bf16[64,16,1024]{2,1,0:T(8,128)(2,1)} %all-to-all-done.2, f32[1024]{0:T(1024)S(1)} %add_divide_fusion, bf16[64,16,1024]{2,1,0:T(8,128)(2,1)S(1)} %all-to-all-done, bf16[1,2048,1024]{2,1,0:T(8,128)(2,1)} %all-gather.7.cloned.1.call-done, ...), kind=kOutput, calls=%fused_computation.36 | convolution fusion | flops 4323277824 | bytes 20979712 | tf_op jit(solution)/shard_map/dot_general | solution.py:65
  194.7 0.0 copy-start.9
  194.7 0.0 copy-done.6
  194.7 0.0 copy-done.7
  194.7 9.6 %fusion.6 = bf16[1024,2048]{1,0:T(8,128)(2,1)S(1)} fusion(f32[1024,2048]{1,0:T(8,128)S(1)} %copy-done.7, bf16[1024,1024]{1,0:T(8,128)(2,1)S(1)} %get-tuple-element.12, bf16[1,2048,1024]{2,1,0:T(8,128)(2,1)S(1)} %copy-done.6), kind=kOutput, calls=%fused_computation.12 | convolution fusion | flops 4336910336 | bytes 18874368 | tf_op jit(solution)/shard_map/dot_general | solution.py:81
  204.4 0.0 copy-done.9
  204.4 0.0 copy-start.8
  204.4 1.9 copy-done.8
  206.3 7.2 %fusion.39 = f32[2048,1024]{1,0:T(8,128)} fusion(bf16[1024,2048]{1,0:T(8,128)(2,1)S(1)} %fusion.6, bf16[1024,1024]{1,0:T(8,128)(2,1)S(1)} %bitcast.89, f32[1024]{0:T(1024)S(1)} %bitcast.106, f32[1024]{0:T(1024)S(1)} %rsqrt.12), kind=kOutput, calls=%fused_computation.51 | convolution fusion | flops 4299161600 | bytes 14688256 | tf_op jit(solution)/shard_map/dot_general | solution.py:25
  213.5 0.0 reduce-scatter.3.cloned.1.call-update
  213.5 0.3 reduce-scatter.5.cloned.1.call-start
  213.8 13.1 %fusion.52 = f32[2048,1024]{1,0:T(8,128)} fusion(bf16[1024,1024]{1,0:T(8,128)(2,1)} %copy-done.9, f32[1024,2048]{1,0:T(8,128)} %fusion.29), kind=kOutput, calls=%fused_computation.88 | convolution fusion | flops 4313841664 | bytes 18874368 | tf_op jit(solution)/shard_map/dot_general | solution.py:25
  226.8 0.0 reduce-scatter.5.cloned.1.call-update
  226.9 8.3 %all-to-all-start.1 = ((bf16[64,16,1024]{2,1,0:T(8,128)(2,1)}), bf16[64,16,1024]{2,1,0:T(8,128)(2,1)}, u32[]{:S(2)}, u32[]{:S(2)}) async-start(bf16[64,16,1024]{2,1,0:T(8,128)(2,1)} %bitcast.93), calls=%async_computation.1 | async-start | bytes 4194304 | tf_op jit(solution)/shard_map/all_to_all | solution.py:70
  235.2 8.2 %fusion.15 = (f32[1024]{0:T(1024)S(1)}, f32[1024]{0:T(1024)S(1)}, f32[1024,1024]{1,0:T(8,128)S(1)}) fusion(f32[1024]{0:T(1024)S(1)} %rsqrt.12, bf16[64,16,1024]{2,1,0:T(8,128)(2,1)S(1)} %all-to-all-done, f32[1024]{0:T(1024)S(1)} %bitcast.107, bf16[1024,2048]{1,0:T(8,128)(2,1)} %copy-done.8, bf16[1,2048,1024]{2,1,0:T(8,128)(2,1)} %all-gather.5.cloned.1.call-done), kind=kOutput, calls=%fused_computation.29 | convolution fusion | flops 4302305280 | bytes 14696448 | tf_op jit(solution)/shard_map/dot_general | solution.py:83
  243.4 3.9 fusion.21
  247.3 20.9 %all-to-all-done.1 = bf16[64,16,1024]{2,1,0:T(8,128)(2,1)} async-done(((bf16[64,16,1024]{2,1,0:T(8,128)(2,1)}), bf16[64,16,1024]{2,1,0:T(8,128)(2,1)}, u32[]{:S(2)}, u32[]{:S(2)}) %all-to-all-start.1) | async-done | bytes 2097184 | tf_op jit(solution)/shard_map/all_to_all | solution.py:70
  268.2 6.6 %all-to-all-start.3 = ((bf16[64,16,1024]{2,1,0:T(8,128)(2,1)}), bf16[64,16,1024]{2,1,0:T(8,128)(2,1)}, u32[]{:S(2)}, u32[]{:S(2)}) async-start(bf16[64,16,1024]{2,1,0:T(8,128)(2,1)} %bitcast.90), calls=%async_computation.3 | async-start | bytes 4194304 | tf_op jit(solution)/shard_map/all_to_all | solution.py:101
  274.8 0.1 mul.203
  274.9 0.5 fusion.18
  275.4 31.0 %all-reduce = (f32[1,1024]{1,0:T(1,128)}, f32[1,1024]{1,0:T(1,128)}) all-reduce(f32[1,1024]{1,0:T(1,128)S(1)} %bitcast.109, f32[1,1024]{1,0:T(1,128)S(1)} %bitcast.100), channel_id=1, replica_groups=mesh['expert'=64,'dp'=2] {'dp'}, use_global_device_ids=true, to_apply=%region_11.12 | all-reduce | flops 2048 | bytes 16384 | tf_op jit(solution)/shard_map/psum | solution.py:99
  306.3 5.3 %gather_fusion = bf16[512,1024]{1,0:T(8,128)(2,1)} fusion(bf16[1024,1024]{1,0:T(8,128)(2,1)} %bitcast.14, s32[1024]{0:T(1024)S(1)} %pad_clamp_fusion), kind=kCustom, calls=%fused_computation | custom fusion | bytes 2099200 | tf_op jit(solution)/shard_map/gather | solution.py:50
  311.7 0.0 all-to-all-done.3
  311.7 0.0 copy-start.1
  311.7 5.4 %gather_fusion.1 = bf16[512,1024]{1,0:T(8,128)(2,1)} fusion(bf16[1024,1024]{1,0:T(8,128)(2,1)} %bitcast.21, s32[1024]{0:T(1024)S(1)} %pad_clamp_fusion), kind=kCustom, calls=%fused_computation.1 | custom fusion | bytes 2099200 | tf_op jit(solution)/shard_map/gather | solution.py:50
  317.1 44.3 %reduce-scatter.3.cloned.1.call-done = f32[1024,1024]{1,0:T(8,128)} async-done(((f32[2048,1024]{1,0:T(8,128)}), f32[1024,1024]{1,0:T(8,128)}) %reduce-scatter.3.cloned.1.call-update) | async-done | bytes 4194320 | tf_op jit(solution)/shard_map/reduce_scatter | solution.py:84
  361.4 108.9 %reduce-scatter.5.cloned.1.call-done = f32[1024,1024]{1,0:T(8,128)} async-done(((f32[2048,1024]{1,0:T(8,128)}), f32[1024,1024]{1,0:T(8,128)}) %reduce-scatter.5.cloned.1.call-update) | async-done | bytes 4194320 | tf_op jit(solution)/shard_map/reduce_scatter | solution.py:87
  470.3 0.0 copy-done.1
  (13 shorter events, 0.2 us)
Async XLA Ops:
  7.2 3.2 copy-start
  7.2 1.5 copy-start.3
  7.2 111.6 %all-gather.5.cloned.1.call-start = ((), (), s32[]{:S(2)}) async-start(), calls=%async_computation.8 | async-start | bytes 6291456 | tf_op jit(solution)/shard_map/all_gather | solution.py:59
  7.9 175.8 %all-gather.7.cloned.1.call-start = ((), (), s32[]{:S(2)}) async-start(), calls=%async_computation.9 | async-start | bytes 6291456 | tf_op jit(solution)/shard_map/all_gather | solution.py:60
  8.7 16.7 %copy-start.2 = (bf16[1,512,1024]{2,1,0:T(8,128)(2,1)S(1)}, bf16[1,512,1024]{2,1,0:T(8,128)(2,1)}, u32[]{:S(2)}) copy-start(bf16[1,512,1024]{2,1,0:T(8,128)(2,1)} %param.8) | copy-start | bytes 3145732
  14.5 43.6 %all-to-all-start = ((bf16[64,16,1024]{2,1,0:T(8,128)(2,1)}), bf16[64,16,1024]{2,1,0:T(8,128)(2,1)S(1)}, u32[]{:S(2)}, u32[]{:S(2)}) async-start(bf16[64,16,1024]{2,1,0:T(8,128)(2,1)} %bitcast.92), calls=%async_computation | async-start | bytes 4194304 | tf_op jit(solution)/shard_map/all_to_all | solution.py:56
  25.4 40.4 %copy-start.4 = (bf16[1,1024]{1,0:T(2,128)(2,1)S(1)}, bf16[1,1024]{1,0:T(2,128)(2,1)}, u32[]{:S(2)}) copy-start(bf16[1,1024]{1,0:T(2,128)(2,1)} %param.11) | copy-start | bytes 6148
  58.1 60.7 %copy-start.5 = (f32[1,1024]{1,0:T(1,128)S(1)}, f32[1,1024]{1,0:T(1,128)}, u32[]{:S(2)}) copy-start(f32[1,1024]{1,0:T(1,128)} %param.10) | copy-start | bytes 12292
  58.1 69.8 %all-to-all-start.2 = ((bf16[64,16,1024]{2,1,0:T(8,128)(2,1)}), bf16[64,16,1024]{2,1,0:T(8,128)(2,1)}, u32[]{:S(2)}, u32[]{:S(2)}) async-start(bf16[64,16,1024]{2,1,0:T(8,128)(2,1)} %bitcast.91), calls=%async_computation.2 | async-start | bytes 4194304 | tf_op jit(solution)/shard_map/all_to_all | solution.py:74
  64.9 296.5 %reduce-scatter.3.cloned.1.call-start = ((), (), s32[]{:S(2)}) async-start(), calls=%async_computation.6 | async-start | bytes 12582912 | tf_op jit(solution)/shard_map/reduce_scatter | solution.py:84
  183.7 11.0 %copy-start.6 = (bf16[1,2048,1024]{2,1,0:T(8,128)(2,1)S(1)}, bf16[1,2048,1024]{2,1,0:T(8,128)(2,1)}, u32[]{:S(2)}) copy-start(bf16[1,2048,1024]{2,1,0:T(8,128)(2,1)} %all-gather.7.cloned.1.call-done) | copy-start | bytes 12582916
  183.7 11.0 %copy-start.7 = (f32[1024,2048]{1,0:T(8,128)S(1)}, f32[1024,2048]{1,0:T(8,128)}, u32[]{:S(2)}) copy-start(f32[1024,2048]{1,0:T(8,128)} %fusion.29) | copy-start | bytes 25165828
  194.7 9.6 %copy-start.9 = (bf16[1024,1024]{1,0:T(8,128)(2,1)}, bf16[1024,1024]{1,0:T(8,128)(2,1)S(1)}, u32[]{:S(2)}) copy-start(bf16[1024,1024]{1,0:T(8,128)(2,1)S(1)} %get-tuple-element.12) | copy-start | bytes 6291460
  204.4 1.9 copy-start.8
  213.5 256.8 %reduce-scatter.5.cloned.1.call-start = ((), (), s32[]{:S(2)}) async-start(), calls=%async_computation.7 | async-start | bytes 12582912 | tf_op jit(solution)/shard_map/reduce_scatter | solution.py:87
  226.9 41.3 %all-to-all-start.1 = ((bf16[64,16,1024]{2,1,0:T(8,128)(2,1)}), bf16[64,16,1024]{2,1,0:T(8,128)(2,1)}, u32[]{:S(2)}, u32[]{:S(2)}) async-start(bf16[64,16,1024]{2,1,0:T(8,128)(2,1)} %bitcast.93), calls=%async_computation.1 | async-start | bytes 4194304 | tf_op jit(solution)/shard_map/all_to_all | solution.py:70
  268.2 43.5 %all-to-all-start.3 = ((bf16[64,16,1024]{2,1,0:T(8,128)(2,1)}), bf16[64,16,1024]{2,1,0:T(8,128)(2,1)}, u32[]{:S(2)}, u32[]{:S(2)}) async-start(bf16[64,16,1024]{2,1,0:T(8,128)(2,1)} %bitcast.90), calls=%async_computation.3 | async-start | bytes 4194304 | tf_op jit(solution)/shard_map/all_to_all | solution.py:101
  311.7 158.7 %copy-start.1 = (bf16[1,512,1024]{2,1,0:T(8,128)(2,1)S(1)}, bf16[1,512,1024]{2,1,0:T(8,128)(2,1)}, u32[]{:S(2)}) copy-start(bf16[1,512,1024]{2,1,0:T(8,128)(2,1)} %param.7) | copy-start | bytes 3145732
Sparse Core Ops, SparseCore 0:
  9.7 109.0 all-gather.4
  120.5 63.2 all-gather.6
  213.6 147.7 reduce-scatter.2
  364.4 105.8 reduce-scatter.4
where the time goes:
time: 478 us; the launch traced here: 477 us
  waiting for transfers between devices  312 us (65%)
  matrix products  58.7 us (12%)
  starting transfers between devices  33.1 us (7%)
  blocking collectives  31 us (6%)
  local copies, waits for them, and re-layouts  21.4 us (4%)
  between operations  14 us (3%)
  other arithmetic  6.34 us (1%)
    reduce_scatter x1, waiting for transfers between devices, local(): lax.psum_scatter(transposed_product(hid, dbranch), 'dp', scatter_dimensio...  109 us
    all_gather x1, waiting for transfers between devices, local(): lax.all_gather(w_out_own, 'dp', axis=0, tiled=True)  55.8 us
    all_gather x1, waiting for transfers between devices, local(): lax.all_gather(w_in_own, 'dp', axis=0, tiled=True)  52.4 us
    reduce_scatter x1, waiting for transfers between devices, local(): lax.psum_scatter(transposed_product(dpre, normed), 'dp', scatter_dimensio...  44.3 us
    psum x1, blocking collectives, local(): gain_grad, router_grad = lax.psum((gain_part, router_part), 'dp')  31 us
    all_to_all x1, waiting for transfers between devices, local(): lax.all_to_all(pack(tokens[0]), 'expert', split_axis=0, concat_axis=0, ti...  28.6 us
    all_to_all x1, waiting for transfers between devices, local(): lax.all_to_all(y_rows.reshape(experts, cap, width), 'expert', split_axis=...  20.9 us
    dot_general x2, matrix products, transposed_product(): lax.dot_general(left, right, (((0,), (0,)), ((), ())), preferred_element_...  20.2 us
  transfers between devices with their start and end apart: 8, of which 6 were waited for; matrix products, arithmetic and copies ran while one was open for 12% of the time, Pallas kernels for 0%

commit v1 on v0

v1 whole, which is shorter than its diff:
```python
import jax
import jax.numpy as jnp
from jax import lax
from jax.sharding import PartitionSpec as P

EPS = 1e-05
FILL = 64.0
SWAP = ((0, 1), (1, 0))


def gelu_fn(values):
    return jax.nn.gelu(values, approximate=True)


def dot(left, right, dims):
    return lax.dot_general(left, right, (dims, ((), ())), preferred_element_type=jnp.float32)


def swap(values):
    return lax.ppermute(values, "dp", SWAP)


def exchange(buffer, experts):
    rows, width = buffer.shape
    out = lax.all_to_all(
        buffer.reshape(experts, rows // experts, width), "expert", split_axis=0, concat_axis=0, tiled=True
    )
    return out.reshape(rows, width)


def normalize(rows, gain_row):
    xf = rows.astype(jnp.float32)
    inv = lax.rsqrt(jnp.mean(xf * xf, -1, keepdims=True) + EPS)
    unit = xf * inv
    return inv, unit, (unit * gain_row).astype(jnp.bfloat16)


def gate_of(rows, router_row):
    return jax.nn.sigmoid(jnp.dot(rows, router_row, preferred_element_type=jnp.float32))[:, None]


def local(tokens, cotangent, assign, gain, router, w_in, w_out):
    experts = lax.axis_size("expert")
    tok = tokens.shape[1]
    cap = 2 * tok // experts
    slots = experts * cap
    bf = jnp.bfloat16
    target = assign[0] // tok
    onehot = (target[:, None] == jnp.arange(experts, dtype=jnp.int32)[None, :]).astype(jnp.int32)
    rank = jnp.sum((jnp.cumsum(onehot, 0) - onehot) * onehot, 1)
    where = target * cap + rank
    place = (where[:, None] == jnp.arange(slots, dtype=jnp.int32)[None, :]).astype(bf)
    empty = 1.0 - jnp.sum(place.astype(jnp.float32), 0)

    gain_row, router_row = gain[0], router[0]
    win, wout = w_in[0], w_out[0]

    x_pack = (dot(place, tokens[0], ((0,), (0,))) + FILL * empty[:, None]).astype(bf)
    dy_pack = dot(place, cotangent[0], ((0,), (0,))).astype(bf)
    x_buf = exchange(x_pack, experts)
    valid = x_buf[:, 0] < 0.5 * FILL
    pos = jnp.where(valid, jnp.cumsum(valid.astype(jnp.int32)) - 1, -1)
    pick = (pos[None, :] == jnp.arange(tok, dtype=jnp.int32)[:, None]).astype(bf)
    x_own = dot(pick, x_buf, ((1,), (0,))).astype(bf)
    x_peer = swap(x_own)
    dy_buf = exchange(dy_pack, experts)
    dy_own = dot(pick, dy_buf, ((1,), (0,)))
    inv_o, unit_o, normed_o = normalize(x_own, gain_row)
    gate_o = gate_of(x_own, router_row)
    pre_o = dot(normed_o, win, ((1,), (1,)))
    hid_o = gelu_fn(pre_o).astype(bf)
    part_o = dot(hid_o, wout, ((1,), (0,)))
    db_o = (gate_o * dy_own).astype(bf)
    db_p = swap(db_o)

    inv_p, unit_p, normed_p = normalize(x_peer, gain_row)
    pre_p = dot(normed_p, win, ((1,), (1,)))
    hid_p = gelu_fn(pre_p).astype(bf)
    part_p = dot(hid_p, wout, ((1,), (0,))).astype(bf)
    branch = part_o + swap(part_p).astype(jnp.float32)

    def backward(pre, db):
        dhid = dot(db, wout, ((1,), (1,)))
        dpre = jax.vjp(gelu_fn, pre)[1](dhid)[0].astype(bf)
        return dpre, dot(dpre, win, ((1,), (0,)))

    dpre_p, dn_p = backward(pre_p, db_p)
    dn_recv = swap(dn_p.astype(bf))
    dpre_o, dn_o = backward(pre_o, db_o)
    grad_in = dot(dpre_o, normed_o, ((0,), (0,))) + dot(dpre_p, normed_p, ((0,), (0,)))
    grad_out = dot(hid_o, db_o, ((0,), (0,))) + dot(hid_p, db_p, ((0,), (0,)))
    gain_part = jnp.sum(dn_o * unit_o, 0) + jnp.sum(dn_p * unit_p, 0)

    xf = x_own.astype(jnp.float32)
    y_rows = (xf + gate_o * branch).astype(bf)
    y_buf = exchange(dot(pick, y_rows, ((0,), (0,))).astype(bf), experts)
    dlogit = jnp.sum(dy_own * branch, -1, keepdims=True) * gate_o * (1.0 - gate_o)
    router_part = jnp.sum(dlogit * xf, 0)
    small = jnp.stack([gain_part, router_part])
    small = small + swap(small)

    dunit = (dn_o + dn_recv.astype(jnp.float32)) * gain_row
    back = (
        dy_own
        + inv_o * (dunit - unit_o * jnp.mean(dunit * unit_o, -1, keepdims=True))
        + dlogit * router_row.astype(jnp.float32)
    ).astype(bf)
    back_buf = exchange(dot(pick, back, ((0,), (0,))).astype(bf), experts)
    mixed = dot(place, y_buf, ((1,), (0,))).astype(bf)
    input_grad = dot(place, back_buf, ((1,), (0,))).astype(bf)
    return (mixed[None], input_grad[None], grad_in[None], grad_out[None], small[:1], small[1:])


def solution(mesh):
    return jax.shard_map(
        local,
        mesh=mesh,
        in_specs=(
            P("dp", "expert", None),
            P("dp", "expert", None),
            P("dp", "expert"),
            P("expert", None),
            P("expert", None),
            P("expert", "dp", None),
            P("expert", "dp", None),
        ),
        out_specs=(
            P("dp", "expert", None),
            P("dp", "expert", None),
            P("expert", "dp", None),
            P("expert", "dp", None),
            P("expert", None),
            P("expert", None),
        ),
        check_vma=False,
    )
```

time: 478 us -> 258 us (0.54)
  waiting for transfers between devices: 312 us -> 95 us
  local copies, waits for them, and re-layouts: 21.4 us -> 3.97 us
  matrix products: 58.7 us -> 72.8 us
  between operations: 14 us -> 0.92 us
  blocking collectives: 31 us -> 39.7 us
  starting transfers between devices: 33.1 us -> 38.7 us
    reduce_scatter x2 -> x0, waiting for transfers between devices: 153 us -> none  [the longest x1 109 us: local(): lax.psum_scatter(transposed_product(hid, dbranch), 'dp', scatter_dimensio...]
    all_gather x2 -> x0, waiting for transfers between devices: 108 us -> none  [the longest x1 55.8 us: local(): lax.all_gather(w_out_own, 'dp', axis=0, tiled=True)]
    ppermute x0 -> x5, waiting for transfers between devices: none -> 78.9 us  [swap(): return lax.ppermute(values, 'dp', SWAP)]
    all_to_all x0 -> x1, blocking collectives: none -> 39.7 us  [exchange(): lax.all_to_all(buffer.reshape(experts, rows // experts, width), 'expert',...]
    all_to_all x4 -> x3, waiting for transfers between devices: 49.5 us -> 16.1 us  [exchange(): lax.all_to_all(buffer.reshape(experts, rows // experts, width), 'expert',...]
    psum x1 -> x0, blocking collectives: 31 us -> none  [local(): gain_grad, router_grad = lax.psum((gain_part, router_part), 'dp')]
    dot_general x6 -> x20, matrix products: 58.1 us -> 72.4 us  [dot(): lax.dot_general(left, right, (dims, ((), ())), preferred_element_type=jnp...]
    ppermute x0 -> x5, starting transfers between devices: none -> 13.3 us  [swap(): return lax.ppermute(values, 'dp', SWAP)]
  transfers between devices with their start and end apart: 8 -> 8, of which waited for: 6 -> 7; matrix products, arithmetic and copies ran while one was open for 12% -> 20% of each run, Pallas kernels for 0% -> 0%
where the time goes in v1:
time: 258 us; the launch traced here: 257 us
  waiting for transfers between devices  95 us (37%)
  matrix products  72.8 us (28%)
  blocking collectives  39.7 us (15%)
  starting transfers between devices  38.7 us (15%)
  other arithmetic  5.9 us (2%)
  local copies, waits for them, and re-layouts  3.97 us (2%)
    ppermute x5, waiting for transfers between devices, swap(): return lax.ppermute(values, 'dp', SWAP)  78.9 us
    dot_general x20, matrix products, dot(): lax.dot_general(left, right, (dims, ((), ())), preferred_element_type=jnp...  72.4 us
    all_to_all x1, blocking collectives, exchange(): lax.all_to_all(buffer.reshape(experts, rows // experts, width), 'expert',...  39.7 us
    all_to_all x3, starting transfers between devices, exchange(): lax.all_to_all(buffer.reshape(experts, rows // experts, width), 'expert',...  25.4 us
    all_to_all x3, waiting for transfers between devices, exchange(): lax.all_to_all(buffer.reshape(experts, rows // experts, width), 'expert',...  16.1 us
    ppermute x5, starting transfers between devices, swap(): return lax.ppermute(values, 'dp', SWAP)  13.3 us
  transfers between devices with their start and end apart: 8, of which 7 were waited for; matrix products, arithmetic and copies ran while one was open for 20% of the time, Pallas kernels for 0%

profile of v1, /device:TPU:1, one launch (start us, length us, event | category | flops | bytes accessed | tf_op | source)
XLA Modules:
  0.0 256.9 jit_solution(13644135756211086274)
XLA Ops:
  0.6 0.0 copy-start
  0.6 0.8 add_select_fusion
  1.5 0.7 add_select_fusion.1
  2.2 1.2 reduce-window.15
  3.4 0.2 slice_reduce_fusion
  3.7 0.1 fusion.98
  3.8 0.7 multiply_add_fusion
  4.5 0.3 convert_reduce_fusion
  4.8 2.6 %add_convert_fusion = bf16[1024,1024]{1,0:T(8,128)(2,1)S(1)} fusion(f32[1024]{0:T(1024)S(1)} %subtract_multiply_fusion, bf16[1,512,1024]{2,1,0:T(8,128)(2,1)} %param.7, s32[512]{0:T(512)S(1)} %multiply_add_fusion), kind=kOutput, calls=%fused_computation.2 | convolution fusion | flops 1076363264 | bytes 3151872 | tf_op jit(solution)/shard_map/dot_general | solution.py:16
  7.4 39.7 %all_to_all.20 = bf16[64,16,1024]{2,1,0:T(8,128)(2,1)S(1)} all-to-all(bf16[64,16,1024]{2,1,0:T(8,128)(2,1)S(1)} %bitcast.99), channel_id=1, replica_groups=mesh['expert'=64,'dp'=2] {'expert'}, dimensions={0} | all-to-all | bytes 4194304 | tf_op jit(solution)/shard_map/all_to_all | solution.py:25
  47.0 1.3 copy-done.1
  48.4 0.1 slice.30
  48.4 0.1 copy.18
  48.6 0.3 reduce-window.19
  48.9 0.1 slice.25
  49.0 0.1 slice_reduce_fusion.1
  49.1 0.1 bitcast_select_fusion
  49.2 3.0 %fusion.31 = (f32[512]{0:T(512)S(1)}, bf16[512,1024]{1,0:T(8,128)(2,1)S(1)}) fusion(bf16[1024,1024]{1,0:T(8,128)(2,1)} %bitcast.95, s32[1024]{0:T(1024)S(1)} %bitcast_select_fusion), kind=kOutput, calls=%fused_computation.44 | convolution fusion | flops 1076362752 | bytes 3151872 | tf_op jit(solution)/shard_map/dot_general | solution.py:16
  52.2 2.7 %collective-permute-start = (bf16[512,1024]{1,0:T(8,128)(2,1)S(1)}, bf16[512,1024]{1,0:T(8,128)(2,1)}, u32[]{:S(2)}, u32[]{:S(2)}) collective-permute-start(bf16[512,1024]{1,0:T(8,128)(2,1)S(1)} %get-tuple-element.18), channel_id=1, source_target_pairs={{0,1},{1,0},{2,3},{3,2},{4,5},{5,4},{6,7},{7,6},{8,9},{9,8},{10,11... | collective-permute-start | bytes 3145736 | tf_op jit(solution)/shard_map/ppermute | solution.py:20
  54.9 2.7 %fusion.58 = bf16[1024,1024]{1,0:T(8,128)(2,1)} fusion(bf16[1,512,1024]{2,1,0:T(8,128)(2,1)S(1)} %copy-done.10, s32[512]{0:T(512)S(1)} %multiply_add_fusion), kind=kOutput, calls=%fused_computation.80 | convolution fusion | flops 1075314688 | bytes 3147776 | tf_op jit(solution)/shard_map/dot_general | solution.py:16
  57.6 5.5 %all-to-all-start.2 = ((bf16[64,16,1024]{2,1,0:T(8,128)(2,1)}), bf16[64,16,1024]{2,1,0:T(8,128)(2,1)}, u32[]{:S(2)}, u32[]{:S(2)}) async-start(bf16[64,16,1024]{2,1,0:T(8,128)(2,1)} %bitcast.98), calls=%async_computation.2 | async-start | bytes 4194304 | tf_op jit(solution)/shard_map/all_to_all | solution.py:25
  63.2 0.0 copy-start.6
  63.2 0.4 fusion.100
  63.5 31.8 %collective-permute-done = bf16[512,1024]{1,0:T(8,128)(2,1)} collective-permute-done((bf16[512,1024]{1,0:T(8,128)(2,1)S(1)}, bf16[512,1024]{1,0:T(8,128)(2,1)}, u32[]{:S(2)}, u32[]{:S(2)}) %collective-permute-start) | collective-permute-done | bytes 1048608 | tf_op jit(solution)/shard_map/ppermute | solution.py:20
  95.3 1.5 fusion.8
  96.9 0.0 copy-start.8
  96.9 2.7 %fusion.46 = f32[512,1024]{1,0:T(8,128)S(1)} fusion(bf16[1,1024,1024]{2,1,0:T(8,128)(2,1)S(1)} %copy-done, bf16[512,1024]{1,0:T(8,128)(2,1)} %collective-permute-done, f32[512]{0:T(512)S(1)} %add_rsqrt_fusion, f32[1024]{0:T(1024)S(1)} %bitcast.107), kind=kOutput, calls=%fused_computation.59 | convolution fusion | flops 1075838976 | bytes 5249024 | tf_op jit(solution)/shard_map/dot_general | solution.py:16
  99.6 2.4 fusion.68
  102.0 2.6 %collective-permute-start.1 = (bf16[512,1024]{1,0:T(8,128)(2,1)}, bf16[512,1024]{1,0:T(8,128)(2,1)}, u32[]{:S(2)}, u32[]{:S(2)}) collective-permute-start(bf16[512,1024]{1,0:T(8,128)(2,1)} %fusion.68), channel_id=1, source_target_pairs={{0,1},{1,0},{2,3},{3,2},{4,5},{5,4},{6,7},{7,6},{8,9},{9,8},{10,11... | collective-permute-start | bytes 3145736 | tf_op jit(solution)/shard_map/ppermute | solution.py:20
  104.6 1.3 fusion.48
  105.9 1.3 copy-done.15
  107.3 2.8 %fusion.40 = f32[512,1024]{1,0:T(8,128)} fusion(bf16[1,1024,1024]{2,1,0:T(8,128)(2,1)S(1)} %copy-done.8, f32[512,1024]{1,0:T(8,128)S(1)} %fusion.48), kind=kOutput, calls=%fused_computation.53 | convolution fusion | flops 1078460416 | bytes 6291456 | tf_op jit(solution)/shard_map/dot_general | solution.py:16
  110.0 0.0 all-to-all-done.2
  110.0 16.8 %collective-permute-done.1 = bf16[512,1024]{1,0:T(8,128)(2,1)} collective-permute-done((bf16[512,1024]{1,0:T(8,128)(2,1)}, bf16[512,1024]{1,0:T(8,128)(2,1)}, u32[]{:S(2)}, u32[]{:S(2)}) %collective-permute-start.1) | collective-permute-done | bytes 1048608 | tf_op jit(solution)/shard_map/ppermute | solution.py:20
  126.8 5.5 %multiply_reduce_fusion = (f32[512]{0:T(512)S(1)}, bf16[512,1024]{1,0:T(8,128)(2,1)}, f32[512,1024]{1,0:T(8,128)}) fusion(f32[512,1024]{1,0:T(8,128)} %fusion.40, bf16[512,1024]{1,0:T(8,128)(2,1)} %collective-permute-done.1, f32[512]{0:T(512)S(1)} %add_divide_fusion, bf16[1024,1024]{1,0:T(8,128)(2,1)} %bitcast.17, s32[1024]{0:T(1024)S(1)} %bitcast_select_fusion), kind=kOutput, calls=%fused_computation.63 | convolution fusion | flops 1077411328 | bytes 8396800 | tf_op jit(solution)/shard_map/dot_general | solution.py:16
  132.3 2.6 %collective-permute-start.2 = (bf16[512,1024]{1,0:T(8,128)(2,1)}, bf16[512,1024]{1,0:T(8,128)(2,1)}, u32[]{:S(2)}, u32[]{:S(2)}) collective-permute-start(bf16[512,1024]{1,0:T(8,128)(2,1)} %get-tuple-element.12), channel_id=1, source_target_pairs={{0,1},{1,0},{2,3},{3,2},{4,5},{5,4},{6,7},{7,6},{8,9},{9,8},{10,11... | collective-permute-start | bytes 3145736 | tf_op jit(solution)/shard_map/ppermute | solution.py:20
  135.0 0.0 copy-start.9
  135.0 4.8 %fusion.59 = bf16[1024,1024]{1,0:T(8,128)(2,1)} fusion(bf16[512,1024]{1,0:T(8,128)(2,1)S(1)} %get-tuple-element.18, f32[512,1024]{1,0:T(8,128)} %fusion.40, bf16[512,1024]{1,0:T(8,128)(2,1)} %collective-permute-done.1, f32[512]{0:T(512)S(1)} %add_divide_fusion, s32[1024]{0:T(1024)S(1)} %bitcast_select_fusion), kind=kOutput, calls=%fused_computation.81 | convolution fusion | flops 1078460416 | bytes 6297600 | tf_op jit(solution)/shard_map/dot_general | solution.py:16
  139.8 16.4 %collective-permute-done.2 = bf16[512,1024]{1,0:T(8,128)(2,1)} collective-permute-done((bf16[512,1024]{1,0:T(8,128)(2,1)}, bf16[512,1024]{1,0:T(8,128)(2,1)}, u32[]{:S(2)}, u32[]{:S(2)}) %collective-permute-start.2) | collective-permute-done | bytes 1048608 | tf_op jit(solution)/shard_map/ppermute | solution.py:20
  156.3 0.0 copy-done.13
  156.3 3.6 %fusion.22 = bf16[512,1024]{1,0:T(8,128)(2,1)S(1)} fusion(f32[512,1024]{1,0:T(8,128)S(1)} %copy-done.13, bf16[512,1024]{1,0:T(8,128)(2,1)} %collective-permute-done.2, bf16[1,1024,1024]{2,1,0:T(8,128)(2,1)S(1)} %copy-done.9), kind=kOutput, calls=%fused_computation.35 | convolution fusion | flops 1084227584 | bytes 6291456 | tf_op jit(solution)/shard_map/dot_general | solution.py:16
  159.9 3.9 %fusion.7 = (f32[1024]{0:T(1024)S(1)}, bf16[512,1024]{1,0:T(8,128)(2,1)}) fusion(bf16[512,1024]{1,0:T(8,128)(2,1)} %collective-permute-done, f32[512]{0:T(512)S(1)} %add_rsqrt_fusion, bf16[512,1024]{1,0:T(8,128)(2,1)S(1)} %fusion.22, bf16[1,1024,1024]{2,1,0:T(8,128)(2,1)S(1)} %copy-done), kind=kOutput, calls=%fused_computation.20 | convolution fusion | flops 1076362240 | bytes 5249024 | tf_op jit(solution)/shard_map/dot_general | solution.py:16
  163.8 0.0 copy-done.4
  163.8 2.6 %collective-permute-start.3 = (bf16[512,1024]{1,0:T(8,128)(2,1)}, bf16[512,1024]{1,0:T(8,128)(2,1)}, u32[]{:S(2)}, u32[]{:S(2)}) collective-permute-start(bf16[512,1024]{1,0:T(8,128)(2,1)} %get-tuple-element.10), channel_id=1, source_target_pairs={{0,1},{1,0},{2,3},{3,2},{4,5},{5,4},{6,7},{7,6},{8,9},{9,8},{10,11... | collective-permute-start | bytes 3145736 | tf_op jit(solution)/shard_map/ppermute | solution.py:20
  166.4 4.7 %fusion.107 = f32[1024,1024]{1,0:T(8,128)} fusion(bf16[512,1024]{1,0:T(8,128)(2,1)} %get-tuple-element.12, f32[512,1024]{1,0:T(8,128)S(1)} %copy-done.16), kind=kOutput, calls=%fused_computation.144 | convolution fusion | flops 1078460416 | bytes 7340032 | tf_op jit(solution)/shard_map/dot_general | solution.py:16
  171.1 8.7 %all-to-all-start.1 = ((bf16[64,16,1024]{2,1,0:T(8,128)(2,1)}), bf16[64,16,1024]{2,1,0:T(8,128)(2,1)}, u32[]{:S(2)}, u32[]{:S(2)}) async-start(bf16[64,16,1024]{2,1,0:T(8,128)(2,1)} %bitcast.97), calls=%async_computation.1 | async-start | bytes 4194304 | tf_op jit(solution)/shard_map/all_to_all | solution.py:25
  179.8 4.9 %fusion.15 = bf16[512,1024]{1,0:T(8,128)(2,1)S(1)} fusion(f32[512,1024]{1,0:T(8,128)} %copy-done.15, bf16[512,1024]{1,0:T(8,128)(2,1)} %get-tuple-element.12, bf16[1,1024,1024]{2,1,0:T(8,128)(2,1)} %param.13), kind=kOutput, calls=%fused_computation.28 | convolution fusion | flops 1084227584 | bytes 6291456 | tf_op jit(solution)/shard_map/dot_general | solution.py:16
  184.7 0.0 copy-start.3
  184.7 13.0 %collective-permute-done.3 = bf16[512,1024]{1,0:T(8,128)(2,1)} collective-permute-done((bf16[512,1024]{1,0:T(8,128)(2,1)}, bf16[512,1024]{1,0:T(8,128)(2,1)}, u32[]{:S(2)}, u32[]{:S(2)}) %collective-permute-start.3) | collective-permute-done | bytes 1048608 | tf_op jit(solution)/shard_map/ppermute | solution.py:20
  197.7 3.0 %fusion.30 = (f32[1024]{0:T(1024)S(1)}, f32[512]{0:T(512)S(1)}, f32[1024]{0:T(1024)S(1)}, f32[512,1024]{1,0:T(8,128)S(1)}) fusion(bf16[512,1024]{1,0:T(8,128)(2,1)S(1)} %get-tuple-element.18, f32[512]{0:T(512)S(1)} %add_rsqrt_fusion.1, f32[1024]{0:T(1024)S(1)} %bitcast.109, bf16[512,1024]{1,0:T(8,128)(2,1)} %collective-permute-done.3, ...), kind=kOutput, calls=%fused_computation.43 | convolution fusion | flops 1079506432 | bytes 7358464 | tf_op jit(solution)/shard_map/dot_general | solution.py:16
  200.7 4.4 %fusion.60 = bf16[1024,1024]{1,0:T(8,128)(2,1)} fusion(f32[512,1024]{1,0:T(8,128)S(1)} %copy-done.2, bf16[512,1024]{1,0:T(8,128)(2,1)S(1)} %get-tuple-element.18, f32[512,1024]{1,0:T(8,128)S(1)} %get-tuple-element.21, bf16[512,1024]{1,0:T(8,128)(2,1)} %collective-permute-done.3, f32[1024]{0:T(1024)S(1)} %mul.278, f32[512]{0:T(512)S(1)} %subtract_multiply_fusion.1, ...), kind=kOutput, calls=%fused_computation.82 | convolution fusion | flops 1081606144 | bytes 8407040 | tf_op jit(solution)/shard_map/dot_general | solution.py:16
  205.2 7.7 %all-to-all-done.1 = bf16[64,16,1024]{2,1,0:T(8,128)(2,1)} async-done(((bf16[64,16,1024]{2,1,0:T(8,128)(2,1)}), bf16[64,16,1024]{2,1,0:T(8,128)(2,1)}, u32[]{:S(2)}, u32[]{:S(2)}) %all-to-all-start.1) | async-done | bytes 2097184 | tf_op jit(solution)/shard_map/all_to_all | solution.py:25
  212.9 11.2 %all-to-all-start.3 = ((bf16[64,16,1024]{2,1,0:T(8,128)(2,1)}), bf16[64,16,1024]{2,1,0:T(8,128)(2,1)}, u32[]{:S(2)}, u32[]{:S(2)}) async-start(bf16[64,16,1024]{2,1,0:T(8,128)(2,1)} %bitcast.96), calls=%async_computation.3 | async-start | bytes 4194304 | tf_op jit(solution)/shard_map/all_to_all | solution.py:25
  224.1 0.0 copy-start.5
  224.1 2.7 %fusion.91 = f32[1024,1024]{1,0:T(8,128)S(1)} fusion(bf16[512,1024]{1,0:T(8,128)(2,1)} %copy-done.3, bf16[512,1024]{1,0:T(8,128)(2,1)S(1)} %get-tuple-element.18, f32[1024]{0:T(1024)S(1)} %bitcast.111, f32[512]{0:T(512)S(1)} %add_rsqrt_fusion.1), kind=kOutput, calls=%fused_computation.105 | convolution fusion | flops 1075838976 | bytes 6297600 | tf_op jit(solution)/shard_map/dot_general | solution.py:16
  226.8 0.0 copy-start.11
  226.9 4.9 %add_bitcast_fusion.1 = f32[1,1024,1024]{2,1,0:T(8,128)} fusion(f32[1024,1024]{1,0:T(8,128)S(1)} %fusion.91, bf16[512,1024]{1,0:T(8,128)(2,1)S(1)} %copy-done.5, bf16[512,1024]{1,0:T(8,128)(2,1)} %collective-permute-done, f32[512]{0:T(512)S(1)} %add_rsqrt_fusion, f32[1024]{0:T(1024)S(1)} %bitcast.112), kind=kOutput, calls=%fused_computation.1 | convolution fusion | flops 1076887552 | bytes 10491904 | tf_op jit(solution)/shard_map/dot_general | solution.py:16
  231.8 4.9 %add_bitcast_fusion = f32[1,1024,1024]{2,1,0:T(8,128)} fusion(f32[1024,1024]{1,0:T(8,128)S(1)} %copy-done.11, bf16[512,1024]{1,0:T(8,128)(2,1)} %collective-permute-done.2, f32[512,1024]{1,0:T(8,128)S(1)} %copy-done.14), kind=kOutput, calls=%fused_computation | convolution fusion | flops 1079508992 | bytes 11534336 | tf_op jit(solution)/shard_map/dot_general | solution.py:16
  236.6 2.7 %collective-permute-start.4 = (f32[2,1024]{1,0:T(2,128)S(1)}, f32[2,1024]{1,0:T(2,128)S(1)}, u32[]{:S(2)}, u32[]{:S(2)}) collective-permute-start(f32[2,1024]{1,0:T(2,128)S(1)} %pad_maximum_fusion), channel_id=1, source_target_pairs={{0,1},{1,0},{2,3},{3,2},{4,5},{5,4},{6,7},{7,6},{8,9},{9,8},{10,11... | collective-permute-start | bytes 24584 | tf_op jit(solution)/shard_map/ppermute | solution.py:20
  239.3 3.9 %fusion.72 = bf16[1,512,1024]{2,1,0:T(8,128)(2,1)} fusion(bf16[1024,1024]{1,0:T(8,128)(2,1)} %bitcast.13, s32[512]{0:T(512)S(1)} %multiply_add_fusion), kind=kOutput, calls=%fused_computation.88 | convolution fusion | flops 1074790400 | bytes 3147776 | tf_op jit(solution)/shard_map/dot_general | solution.py:16
  243.2 0.8 collective-permute-done.4
  244.0 0.6 fusion.108
  244.7 8.4 %all-to-all-done.3 = bf16[64,16,1024]{2,1,0:T(8,128)(2,1)} async-done(((bf16[64,16,1024]{2,1,0:T(8,128)(2,1)}), bf16[64,16,1024]{2,1,0:T(8,128)(2,1)}, u32[]{:S(2)}, u32[]{:S(2)}) %all-to-all-start.3) | async-done | bytes 2097184 | tf_op jit(solution)/shard_map/all_to_all | solution.py:25
  253.0 3.9 %fusion.71 = bf16[1,512,1024]{2,1,0:T(8,128)(2,1)} fusion(bf16[1024,1024]{1,0:T(8,128)(2,1)} %bitcast.19, s32[512]{0:T(512)S(1)} %multiply_add_fusion), kind=kOutput, calls=%fused_computation.87 | convolution fusion | flops 1074790400 | bytes 3147776 | tf_op jit(solution)/shard_map/dot_general | solution.py:16
  (39 shorter events, 0.3 us)
Async XLA Ops:
  0.6 96.2 %copy-start = (bf16[1,1024,1024]{2,1,0:T(8,128)(2,1)S(1)}, bf16[1,1024,1024]{2,1,0:T(8,128)(2,1)}, u32[]{:S(2)}) copy-start(bf16[1,1024,1024]{2,1,0:T(8,128)(2,1)} %param.12) | copy-start | bytes 6291460
  47.0 1.3 copy-start.1
  49.2 5.7 %copy-start.10 = (bf16[1,512,1024]{2,1,0:T(8,128)(2,1)S(1)}, bf16[1,512,1024]{2,1,0:T(8,128)(2,1)}, u32[]{:S(2)}) copy-start(bf16[1,512,1024]{2,1,0:T(8,128)(2,1)} %param.8) | copy-start | bytes 3145732
  52.2 43.1 %collective-permute-start = (bf16[512,1024]{1,0:T(8,128)(2,1)S(1)}, bf16[512,1024]{1,0:T(8,128)(2,1)}, u32[]{:S(2)}, u32[]{:S(2)}) collective-permute-start(bf16[512,1024]{1,0:T(8,128)(2,1)S(1)} %get-tuple-element.18), channel_id=1, source_target_pairs={{0,1},{1,0},{2,3},{3,2},{4,5},{5,4},{6,7},{7,6},{8,9},{9,8},{10,11... | collective-permute-start | bytes 3145736 | tf_op jit(solution)/shard_map/ppermute | solution.py:20
  57.6 5.5 %copy-start.7 = (bf16[1,1024]{1,0:T(2,128)(2,1)S(1)}, bf16[1,1024]{1,0:T(2,128)(2,1)}, u32[]{:S(2)}) copy-start(bf16[1,1024]{1,0:T(2,128)(2,1)} %param.11) | copy-start | bytes 6148
  57.6 52.4 %all-to-all-start.2 = ((bf16[64,16,1024]{2,1,0:T(8,128)(2,1)}), bf16[64,16,1024]{2,1,0:T(8,128)(2,1)}, u32[]{:S(2)}, u32[]{:S(2)}) async-start(bf16[64,16,1024]{2,1,0:T(8,128)(2,1)} %bitcast.98), calls=%async_computation.2 | async-start | bytes 4194304 | tf_op jit(solution)/shard_map/all_to_all | solution.py:25
  63.2 33.7 %copy-start.6 = (f32[1,1024]{1,0:T(1,128)S(1)}, f32[1,1024]{1,0:T(1,128)}, u32[]{:S(2)}) copy-start(f32[1,1024]{1,0:T(1,128)} %param.10) | copy-start | bytes 12292
  96.9 2.7 %copy-start.8 = (bf16[1,1024,1024]{2,1,0:T(8,128)(2,1)S(1)}, bf16[1,1024,1024]{2,1,0:T(8,128)(2,1)}, u32[]{:S(2)}) copy-start(bf16[1,1024,1024]{2,1,0:T(8,128)(2,1)} %param.13) | copy-start | bytes 6291460
  99.5 2.4 copy-start.12
  102.0 24.9 %collective-permute-start.1 = (bf16[512,1024]{1,0:T(8,128)(2,1)}, bf16[512,1024]{1,0:T(8,128)(2,1)}, u32[]{:S(2)}, u32[]{:S(2)}) collective-permute-start(bf16[512,1024]{1,0:T(8,128)(2,1)} %fusion.68), channel_id=1, source_target_pairs={{0,1},{1,0},{2,3},{3,2},{4,5},{5,4},{6,7},{7,6},{8,9},{9,8},{10,11... | collective-permute-start | bytes 3145736 | tf_op jit(solution)/shard_map/ppermute | solution.py:20
  105.9 1.3 copy-start.15
  132.3 23.9 %collective-permute-start.2 = (bf16[512,1024]{1,0:T(8,128)(2,1)}, bf16[512,1024]{1,0:T(8,128)(2,1)}, u32[]{:S(2)}, u32[]{:S(2)}) collective-permute-start(bf16[512,1024]{1,0:T(8,128)(2,1)} %get-tuple-element.12), channel_id=1, source_target_pairs={{0,1},{1,0},{2,3},{3,2},{4,5},{5,4},{6,7},{7,6},{8,9},{9,8},{10,11... | collective-permute-start | bytes 3145736 | tf_op jit(solution)/shard_map/ppermute | solution.py:20
  135.0 21.3 %copy-start.9 = (bf16[1,1024,1024]{2,1,0:T(8,128)(2,1)S(1)}, bf16[1,1024,1024]{2,1,0:T(8,128)(2,1)}, u32[]{:S(2)}) copy-start(bf16[1,1024,1024]{2,1,0:T(8,128)(2,1)} %param.13) | copy-start | bytes 6291460
  135.0 21.3 %copy-start.13 = (f32[512,1024]{1,0:T(8,128)S(1)}, f32[512,1024]{1,0:T(8,128)}, u32[]{:S(2)}) copy-start(f32[512,1024]{1,0:T(8,128)} %copy-done.12) | copy-start | bytes 6291460
  159.8 3.9 %copy-start.4 = (bf16[512,1024]{1,0:T(8,128)(2,1)}, bf16[512,1024]{1,0:T(8,128)(2,1)S(1)}, u32[]{:S(2)}) copy-start(bf16[512,1024]{1,0:T(8,128)(2,1)S(1)} %fusion.22) | copy-start | bytes 3145732
  159.9 6.5 %copy-start.16 = (f32[512,1024]{1,0:T(8,128)S(1)}, f32[512,1024]{1,0:T(8,128)}, u32[]{:S(2)}) copy-start(f32[512,1024]{1,0:T(8,128)} %copy-done.15) | copy-start | bytes 6291460
  163.8 33.9 %collective-permute-start.3 = (bf16[512,1024]{1,0:T(8,128)(2,1)}, bf16[512,1024]{1,0:T(8,128)(2,1)}, u32[]{:S(2)}, u32[]{:S(2)}) collective-permute-start(bf16[512,1024]{1,0:T(8,128)(2,1)} %get-tuple-element.10), channel_id=1, source_target_pairs={{0,1},{1,0},{2,3},{3,2},{4,5},{5,4},{6,7},{7,6},{8,9},{9,8},{10,11... | collective-permute-start | bytes 3145736 | tf_op jit(solution)/shard_map/ppermute | solution.py:20
  171.1 41.8 %all-to-all-start.1 = ((bf16[64,16,1024]{2,1,0:T(8,128)(2,1)}), bf16[64,16,1024]{2,1,0:T(8,128)(2,1)}, u32[]{:S(2)}, u32[]{:S(2)}) async-start(bf16[64,16,1024]{2,1,0:T(8,128)(2,1)} %bitcast.97), calls=%async_computation.1 | async-start | bytes 4194304 | tf_op jit(solution)/shard_map/all_to_all | solution.py:25
  184.7 16.0 %copy-start.3 = (bf16[512,1024]{1,0:T(8,128)(2,1)}, bf16[512,1024]{1,0:T(8,128)(2,1)S(1)}, u32[]{:S(2)}) copy-start(bf16[512,1024]{1,0:T(8,128)(2,1)S(1)} %fusion.15) | copy-start | bytes 3145732
  184.7 16.0 %copy-start.2 = (f32[512,1024]{1,0:T(8,128)S(1)}, f32[512,1024]{1,0:T(8,128)}, u32[]{:S(2)}) copy-start(f32[512,1024]{1,0:T(8,128)} %get-tuple-element.19) | copy-start | bytes 6291460
  212.9 40.1 %all-to-all-start.3 = ((bf16[64,16,1024]{2,1,0:T(8,128)(2,1)}), bf16[64,16,1024]{2,1,0:T(8,128)(2,1)}, u32[]{:S(2)}, u32[]{:S(2)}) async-start(bf16[64,16,1024]{2,1,0:T(8,128)(2,1)} %bitcast.96), calls=%async_computation.3 | async-start | bytes 4194304 | tf_op jit(solution)/shard_map/all_to_all | solution.py:25
  224.1 2.7 %copy-start.5 = (bf16[512,1024]{1,0:T(8,128)(2,1)S(1)}, bf16[512,1024]{1,0:T(8,128)(2,1)}, u32[]{:S(2)}) copy-start(bf16[512,1024]{1,0:T(8,128)(2,1)} %copy-done.4) | copy-start | bytes 3145732
  226.8 4.9 %copy-start.11 = (f32[1024,1024]{1,0:T(8,128)S(1)}, f32[1024,1024]{1,0:T(8,128)}, u32[]{:S(2)}) copy-start(f32[1024,1024]{1,0:T(8,128)} %fusion.107) | copy-start | bytes 12582916
  226.9 4.9 %copy-start.14 = (f32[512,1024]{1,0:T(8,128)S(1)}, f32[512,1024]{1,0:T(8,128)}, u32[]{:S(2)}) copy-start(f32[512,1024]{1,0:T(8,128)} %copy-done.12) | copy-start | bytes 6291460
  236.6 7.4 %collective-permute-start.4 = (f32[2,1024]{1,0:T(2,128)S(1)}, f32[2,1024]{1,0:T(2,128)S(1)}, u32[]{:S(2)}, u32[]{:S(2)}) collective-permute-start(f32[2,1024]{1,0:T(2,128)S(1)} %pad_maximum_fusion), channel_id=1, source_target_pairs={{0,1},{1,0},{2,3},{3,2},{4,5},{5,4},{6,7},{7,6},{8,9},{9,8},{10,11... | collective-permute-start | bytes 24584 | tf_op jit(solution)/shard_map/ppermute | solution.py:20

commit v2 on v1

v2 whole, which is shorter than its diff:
```python
import functools

import jax
import jax.numpy as jnp
from jax import lax
from jax.experimental import pallas as pl
from jax.experimental.pallas import tpu as pltpu
from jax.sharding import PartitionSpec as P

EPS = 1e-05
FILL = 64.0
SWAP = ((0, 1), (1, 0))
BF = jnp.bfloat16
F32 = jnp.float32
MIB = 1024 * 1024
TAIL = 16
GF = 10**12


def dot(left, right, dims):
    return lax.dot_general(left, right, (dims, ((), ())), preferred_element_type=F32)


def iota(shape, dim):
    return lax.broadcasted_iota(jnp.int32, shape, dim)


def mask(cond):
    return jnp.where(cond, 1.0, 0.0).astype(BF)


def gate_of(xf, router):
    return jax.nn.sigmoid(jnp.sum(xf * router, -1, keepdims=True))


def inv_of(xf):
    return lax.rsqrt(jnp.mean(xf * xf, -1, keepdims=True) + EPS)


def gelu_and_slope(pre):
    root = 0.7978845608028654
    square = pre * pre
    wave = jnp.tanh(pre * (root + root * 0.044715 * square))
    half = 0.5 + 0.5 * wave
    slope = half + pre * (0.5 - 0.5 * wave * wave) * (root + root * 0.134145 * square)
    return pre * half, slope


def pack_kernel(experts, cap, assign_ref, x_ref, dy_ref, out_ref, slot_ref):
    tok, width = x_ref.shape
    slots = experts * cap
    target = jnp.right_shift(assign_ref[...], tok.bit_length() - 1)
    chosen = mask(iota((experts, tok), 0) == target)
    earlier = mask(iota((tok, tok), 0) < iota((tok, tok), 1))
    ahead = dot(chosen, earlier, ((1,), (0,)))
    rank = jnp.sum(ahead * chosen.astype(F32), 0, keepdims=True)
    slot = target * cap + rank.astype(jnp.int32)
    slot_ref[...] = slot
    place = jnp.where(iota((slots, tok), 0) == slot, 1.0, 0.0)
    empty = FILL - FILL * jnp.sum(place, 1, keepdims=True)
    place = place.astype(BF)
    x = (dot(place, x_ref[...], ((1,), (0,))) + empty).astype(BF)
    out_ref[:, :cap, :] = x.reshape(experts, cap, width)
    dy = dot(place, dy_ref[...], ((1,), (0,))).astype(BF)
    out_ref[:, cap:, :] = dy.reshape(experts, cap, width)


def compact_kernel(buf_ref, x_ref, pos_ref):
    experts, cap, width = buf_ref.shape[0], buf_ref.shape[1] // 2, buf_ref.shape[2]
    slots = experts * cap
    tok = x_ref.shape[0]
    lanes = pos_ref.shape[1]
    rows = buf_ref[:, :cap, :].reshape(slots, width)
    valid = rows[:, :lanes].astype(F32)[:, :1] < 0.5 * FILL
    ones = jnp.broadcast_to(jnp.where(valid, 1.0, 0.0), (slots, lanes))
    bits = cap.bit_length() - 1
    member = mask(jnp.right_shift(iota((experts, slots), 1), bits) == iota((experts, slots), 0))
    counts = dot(member, ones.astype(BF), ((1,), (0,))).astype(BF)
    before = mask(iota((slots, experts), 1) < jnp.right_shift(iota((slots, experts), 0), bits))
    pos = dot(before, counts, ((1,), (0,)))
    pos = pos + jnp.bitwise_and(iota((slots, lanes), 0), cap - 1).astype(F32)
    pos = jnp.where(ones > 0.5, pos, -1.0)
    pos_ref[...] = pos
    pick = mask(iota((tok, slots), 0).astype(F32) == pos.T[:1])
    x_ref[...] = dot(pick, rows, ((1,), (0,))).astype(BF)


def compact_dy_kernel(buf_ref, pos_ref, x_ref, router_ref, dy_ref, db_ref):
    experts, cap, width = buf_ref.shape[0], buf_ref.shape[1] // 2, buf_ref.shape[2]
    tok, slots = x_ref.shape[0], experts * cap
    pick = mask(iota((tok, slots), 0).astype(F32) == pos_ref[...].T[:1])
    dy = dot(pick, buf_ref[:, cap:, :].reshape(slots, width), ((1,), (0,)))
    dy_ref[...] = dy.astype(BF)
    gate = gate_of(x_ref[...].astype(F32), router_ref[...].astype(F32))
    db_ref[...] = (gate * dy).astype(BF)


def forward(x_ref, gain_ref, win_ref, wout_ref, normed_ref, hid_ref):
    xf = x_ref[...].astype(F32)
    normed = (xf * inv_of(xf) * gain_ref[...]).astype(BF)
    normed_ref[...] = normed
    act, slope = gelu_and_slope(dot(normed, win_ref[...], ((1,), (1,))))
    hid = act.astype(BF)
    hid_ref[...] = hid
    return slope, dot(hid, wout_ref[...], ((1,), (0,)))


def backward(x_ref, db_ref, slope, part, gain_ref, router_ref, win_ref, wout_ref, dpre_ref):
    dpre = (slope * dot(db_ref[...], wout_ref[...], ((1,), (1,)))).astype(BF)
    dpre_ref[...] = dpre
    dnormed = dot(dpre, win_ref[...], ((1,), (0,)))
    xf = x_ref[...].astype(F32)
    router = router_ref[...].astype(F32)
    inv = inv_of(xf)
    unit = xf * inv
    dunit = dnormed * gain_ref[...]
    dlogit = (1.0 - gate_of(xf, router)) * jnp.sum(db_ref[...].astype(F32) * part, -1, keepdims=True)
    back = inv * (dunit - unit * jnp.mean(dunit * unit, -1, keepdims=True)) + dlogit * router
    return back, jnp.sum(dnormed * unit, 0, keepdims=True), jnp.sum(dlogit * xf, 0, keepdims=True)


def own_kernel(
    x_ref, db_ref, dy_ref, gain_ref, router_ref, win_ref, wout_ref,
    normed_ref, hid_ref, dpre_ref, part_ref, back_ref, small_ref,
):
    slope, part = forward(x_ref, gain_ref, win_ref, wout_ref, normed_ref, hid_ref)
    part_ref[...] = part
    back, gain_part, router_part = backward(
        x_ref, db_ref, slope, part, gain_ref, router_ref, win_ref, wout_ref, dpre_ref
    )
    back_ref[...] = back + dy_ref[...].astype(F32)
    small_ref[:1, :] = gain_part
    small_ref[1:, :] = router_part


def peer_forward_kernel(x_ref, gain_ref, win_ref, wout_ref, normed_ref, hid_ref, slope_ref, part_ref):
    slope, part = forward(x_ref, gain_ref, win_ref, wout_ref, normed_ref, hid_ref)
    slope_ref[...] = slope.astype(BF)
    part_ref[...] = part.astype(BF)


def peer_backward_kernel(
    x_ref, db_ref, slope_ref, part_ref, small_ref, gain_ref, router_ref, win_ref, wout_ref,
    dpre_ref, back_ref,
):
    tok = x_ref.shape[0]
    back, gain_part, router_part = backward(
        x_ref, db_ref, slope_ref[...].astype(F32), part_ref[...].astype(F32),
        gain_ref, router_ref, win_ref, wout_ref, dpre_ref,
    )
    back_ref[:tok, :] = back.astype(BF)
    small = small_ref[...] + jnp.concatenate([gain_part, router_part], 0)
    high = small.astype(BF)
    rest = small - high.astype(F32)
    middle = rest.astype(BF)
    low = (rest - middle.astype(F32)).astype(BF)
    pad = jnp.zeros((TAIL - 6, small.shape[1]), F32)
    coded = jnp.concatenate([high.astype(F32), middle.astype(F32), low.astype(F32), pad], 0)
    back_ref[tok:, :] = coded.astype(BF)


def grads_kernel(dpo, dpp, no, np_, ho, hp, bo, bp, gin_ref, gout_ref):
    first = ((0,), (0,))
    gin_ref[...] = dot(dpo[...], no[...], first) + dot(dpp[...], np_[...], first)
    gout_ref[...] = dot(ho[...], bo[...], first) + dot(hp[...], bp[...], first)


def spread(pos_ref, rows, out_ref):
    place = mask(iota((out_ref.shape[0], rows.shape[0]), 1).astype(F32) == pos_ref[:, :1])
    out_ref[...] = dot(place, rows, ((1,), (0,))).astype(BF)


def mix_kernel(x_ref, part_ref, recv_ref, router_ref, pos_ref, out_ref):
    xf = x_ref[...].astype(F32)
    gate = gate_of(xf, router_ref[...].astype(F32))
    rows = (xf + gate * (part_ref[...] + recv_ref[...].astype(F32))).astype(BF)
    spread(pos_ref, rows, out_ref)


def decode(ref, tok):
    coded = ref[tok:, :].astype(F32)
    return coded[0:2] + coded[2:4] + coded[4:6]


def add_kernel(own_ref, sent_ref, recv_ref, pos_ref, out_ref, small_ref):
    tok = own_ref.shape[0]
    rows = (own_ref[...] + recv_ref[:tok, :].astype(F32)).astype(BF)
    spread(pos_ref, rows, out_ref)
    small_ref[...] = decode(sent_ref, tok) + decode(recv_ref, tok)


def unpack_kernel(slot_ref, buf_ref, out_ref):
    slots, tok = buf_ref.shape[0], out_ref.shape[0]
    place = mask(iota((slots, tok), 0) == slot_ref[...])
    out_ref[...] = dot(place, buf_ref[...], ((0,), (0,))).astype(BF)


def call(kernel, name, out_shape, flops, moved, inputs, after=None, vmem=32, **kw):
    if after is not None:
        count = len(inputs)
        inner = kernel

        def kernel(*refs):
            inner(*refs[:count], *refs[count + 1:])

        specs = kw.get("in_specs", [pl.BlockSpec(memory_space=pltpu.VMEM)] * count)
        kw["in_specs"] = [*specs, pl.BlockSpec(memory_space=pl.ANY)]
        inputs = (*inputs, after)
    return pl.pallas_call(
        kernel,
        name=name,
        out_shape=out_shape,
        compiler_params=pltpu.CompilerParams(vmem_limit_bytes=vmem * MIB),
        cost_estimate=pl.CostEstimate(flops=flops, bytes_accessed=moved, transcendentals=0),
        **kw,
    )(*inputs)


def shape(dims, dtype):
    return jax.ShapeDtypeStruct(dims, dtype)


def swap(values):
    return lax.ppermute(values, "dp", SWAP)


def exchange(buffer, experts):
    return lax.all_to_all(buffer, "expert", split_axis=0, concat_axis=0, tiled=True)


def local(tokens, cotangent, assign, gain, router, w_in, w_out):
    experts = lax.axis_size("expert")
    tok, width = tokens.shape[1:]
    cap = 2 * tok // experts
    slots = experts * cap
    win, wout = w_in[0], w_out[0]
    hidden = win.shape[0]
    place_cost = 2 * slots * tok * width
    mm = 2 * tok * width * hidden
    rows_bf = shape((tok, width), BF)
    hid_bf = shape((tok, hidden), BF)
    slots_bf = shape((slots, width), BF)

    packed, slot = call(
        functools.partial(pack_kernel, experts, cap), "pack",
        (shape((experts, 2 * cap, width), BF), shape((1, tok), jnp.int32)),
        2 * place_cost, 6 * MIB, (assign, tokens[0], cotangent[0]),
    )
    buf = exchange(packed, experts)
    x_own, pos = call(
        compact_kernel, "compact_x", (rows_bf, shape((slots, 128), F32)), place_cost, 3 * MIB, (buf,)
    )
    x_peer = swap(x_own)
    dy_own, db_own = call(
        compact_dy_kernel, "compact_dy", (rows_bf, rows_bf), place_cost, 4 * MIB, (buf, pos, x_own, router)
    )
    db_peer = swap(db_own)
    normed_o, hid_o, dpre_o, part_o, back_o, small_o = call(
        own_kernel, "own",
        (rows_bf, hid_bf, hid_bf, shape((tok, width), F32), shape((tok, width), F32), shape((2, width), F32)),
        4 * mm, 14 * MIB, (x_own, db_own, dy_own, gain, router, win, wout),
    )
    normed_p, hid_p, slope_p, part_p = call(
        peer_forward_kernel, "peer_forward", (rows_bf, hid_bf, hid_bf, rows_bf),
        2 * mm, 9 * MIB, (x_peer, gain, win, wout), small_o,
    )
    part_recv = swap(part_p)
    dpre_p, back_p = call(
        peer_backward_kernel, "peer_backward", (hid_bf, shape((tok + TAIL, width), BF)),
        2 * mm, 9 * MIB, (x_peer, db_peer, slope_p, part_p, small_o, gain, router, win, wout),
    )
    back_recv = swap(back_p)
    y_pack = call(
        mix_kernel, "mix", slots_bf, place_cost, 8 * MIB, (x_own, part_o, part_recv, router, pos)
    )
    half = hidden // 2
    left = pl.BlockSpec((tok, half), lambda i: (0, i))
    right = pl.BlockSpec((tok, width), lambda i: (0, 0))
    grad = pl.BlockSpec((half, width), lambda i: (i, 0))
    gin, gout = call(
        grads_kernel, "weight_grads", (shape((hidden, width), F32), shape((hidden, width), F32)),
        GF, 16 * MIB, (dpre_o, dpre_p, normed_o, normed_p, hid_o, hid_p, db_own, db_peer), y_pack,
        grid=(2,),
        in_specs=[left, left, right, right, left, left, right, right],
        out_specs=(grad, grad),
    )
    y_buf = exchange(y_pack.reshape(experts, cap, width), experts).reshape(slots, width)
    back_pack, small = call(
        add_kernel, "add_back", (slots_bf, shape((2, width), F32)), place_cost, 5 * MIB,
        (back_o, back_p, back_recv, pos), gin,
    )
    back_pack, y_buf = lax.optimization_barrier((back_pack, y_buf))
    back_buf = exchange(back_pack.reshape(experts, cap, width), experts).reshape(slots, width)
    mixed = call(unpack_kernel, "unpack", rows_bf, place_cost, 3 * MIB, (slot, y_buf))
    input_grad = call(unpack_kernel, "unpack", rows_bf, place_cost, 3 * MIB, (slot, back_buf), mixed)
    return (mixed[None], input_grad[None], gin[None], gout[None], small[:1], small[1:])


def solution(mesh):
    return jax.shard_map(
        local,
        mesh=mesh,
        in_specs=(
            P("dp", "expert", None),
            P("dp", "expert", None),
            P("dp", "expert"),
            P("expert", None),
            P("expert", None),
            P("expert", "dp", None),
            P("expert", "dp", None),
        ),
        out_specs=(
            P("dp", "expert", None),
            P("dp", "expert", None),
            P("expert", "dp", None),
            P("expert", "dp", None),
            P("expert", None),
            P("expert", None),
        ),
        check_vma=False,
    )
```

time: 258 us -> 229 us (0.89)
  matrix products: 72.8 us -> 0 us
  Pallas kernels: 0 us -> 37.5 us
  blocking collectives: 39.7 us -> 62.1 us
  local copies, waits for them, and re-layouts: 3.97 us -> 21.2 us
  starting transfers between devices: 38.7 us -> 23.9 us
  waiting for transfers between devices: 95 us -> 82.6 us
  other arithmetic: 5.9 us -> 0 us
    dot_general x21 -> x0, matrix products: 72.8 us -> none  [the longest x20 72.4 us: dot(): lax.dot_general(left, right, (dims, ((), ())), preferred_element_type=jnp...]
    pallas_call x0 -> x11, Pallas kernels: none -> 37.5 us  [call(): pl.pallas_call(kernel, name=name, out_shape=out_shape, compiler_params=pl...]
    all_to_all x1, blocking collectives: 39.7 us -> 62.1 us  [exchange(): lax.all_to_all(buffer, 'expert', split_axis=0, concat_axis=0, tiled=True)]
    ppermute x5 -> x4, waiting for transfers between devices: 78.9 us -> 58 us  [swap(): return lax.ppermute(values, 'dp', SWAP)]
    unnamed x35 -> x52, local copies, waits for them, and re-layouts: 2.87 us -> 20.6 us
    all_to_all x3 -> x2, starting transfers between devices: 25.4 us -> 15.3 us  [exchange(): lax.all_to_all(buffer, 'expert', split_axis=0, concat_axis=0, tiled=True)]
    all_to_all x3 -> x2, waiting for transfers between devices: 16.1 us -> 24.6 us  [exchange(): lax.all_to_all(buffer, 'expert', split_axis=0, concat_axis=0, tiled=True)]
    ppermute x5 -> x4, starting transfers between devices: 13.3 us -> 8.55 us  [swap(): return lax.ppermute(values, 'dp', SWAP)]
  transfers between devices with their start and end apart: 8 -> 6, of which waited for: 7 -> 5; matrix products, arithmetic and copies ran while one was open for 20% -> 0% of each run, Pallas kernels for 0% -> 14%
where the time goes in v2:
time: 229 us; the launch traced here: 228 us
  waiting for transfers between devices  82.6 us (36%)
  blocking collectives  62.1 us (27%)
  Pallas kernels  37.5 us (16%)
  starting transfers between devices  23.9 us (10%)
  local copies, waits for them, and re-layouts  21.2 us (9%)
    all_to_all x1, blocking collectives, exchange(): lax.all_to_all(buffer, 'expert', split_axis=0, concat_axis=0, tiled=True)  62.1 us
    ppermute x4, waiting for transfers between devices, swap(): return lax.ppermute(values, 'dp', SWAP)  58 us
    pallas_call x11, Pallas kernels, call(): pl.pallas_call(kernel, name=name, out_shape=out_shape, compiler_params=pl...  37.5 us
    all_to_all x2, waiting for transfers between devices, exchange(): lax.all_to_all(buffer, 'expert', split_axis=0, concat_axis=0, tiled=True)  24.6 us
    unnamed x52, local copies, waits for them, and re-layouts  20.6 us
    all_to_all x2, starting transfers between devices, exchange(): lax.all_to_all(buffer, 'expert', split_axis=0, concat_axis=0, tiled=True)  15.3 us
    ppermute x4, starting transfers between devices, swap(): return lax.ppermute(values, 'dp', SWAP)  8.55 us
  transfers between devices with their start and end apart: 6, of which 5 were waited for; matrix products, arithmetic and copies ran while one was open for 0% of the time, Pallas kernels for 14%

profile of v2, /device:TPU:1, one launch (start us, length us, event | category | flops | bytes accessed | tf_op | source)
XLA Modules:
  0.0 228.1 jit_solution(888109256667242587)
XLA Ops:
  0.6 0.0 copy-start.9
  0.6 1.2 copy-done.9
  1.9 0.0 copy-start.10
  1.9 1.2 copy-done.10
  3.1 0.0 copy-start.15
  3.1 0.7 copy-done.15
  3.8 2.7 %pack.1 = (bf16[64,32,1024]{2,1,0:T(8,128)(2,1)S(1)}, s32[1,512]{1,0:T(1,128)S(1)}) custom-call(s32[1,512]{1,0:T(1,128)S(1)} %copy-done.15, bf16[512,1024]{1,0:T(8,128)(2,1)S(1)} %bitcast.22, bf16[512,1024]{1,0:T(8,128)(2,1)S(1)} %bitcast.23), custom_call_target="tpu_custom_call" | custom-call | flops 2147483648 | bytes 6291456 | tf_op jit(solution)/shard_map/pack/pallas_call | solution.py:209
  6.4 62.1 %all_to_all.15.buf_ref = bf16[64,32,1024]{2,1,0:T(8,128)(2,1)S(1)} all-to-all(bf16[64,32,1024]{2,1,0:T(8,128)(2,1)S(1)} %get-tuple-element.31), channel_id=1, replica_groups=mesh['expert'=64,'dp'=2] {'expert'}, dimensions={0} | all-to-all | bytes 8388608 | tf_op jit(solution)/shard_map/all_to_all | solution.py:228
  68.6 1.8 compact_x.1
  70.3 0.0 copy-start
  70.3 2.7 %collective-permute-start = (bf16[512,1024]{1,0:T(8,128)(2,1)S(1)}, bf16[512,1024]{1,0:T(8,128)(2,1)S(1)}, u32[]{:S(2)}, u32[]{:S(2)}) collective-permute-start(bf16[512,1024]{1,0:T(8,128)(2,1)S(1)} %get-tuple-element.32.x_ref), channel_id=1, source_target_pairs={{0,1},{1,0},{2,3},{3,2},{4,5},{5,4},{6,7},{7,6},{8,9},{9,8},{10,11... | collective-permute-start | bytes 3145736 | tf_op jit(solution)/shard_map/ppermute | solution.py:224
  73.0 0.0 copy-done.7
  73.0 0.0 copy-start.5
  73.0 0.0 copy-start.8
  73.1 1.4 compact_dy.1
  74.4 0.0 copy-start.11
  74.4 0.6 collective-permute-start.1
  75.1 0.0 copy-done.4
  75.1 0.2 copy-done.5
  75.3 0.0 copy-done.8
  75.3 5.9 %own.1 = (bf16[512,1024]{1,0:T(8,128)(2,1)S(1)}, bf16[512,1024]{1,0:T(8,128)(2,1)S(1)}, bf16[512,1024]{1,0:T(8,128)(2,1)S(1)}, f32[512,1024]{1,0:T(8,128)S(1)}, ...) custom-call(bf16[512,1024]{1,0:T(8,128)(2,1)S(1)} %get-tuple-element.32.x_ref, ...), custom_call_target="tpu_custom_call" | custom-call | flops 4294967296 | bytes 14680064 | tf_op jit(solution)/shard_map/own/pallas_call | solution.py:209
  81.1 0.0 copy-done.11
  81.1 0.0 copy-start.20
  81.2 1.0 copy-done.20
  82.1 0.0 copy-start.24
  82.1 1.0 copy-done.24
  83.1 0.0 copy-start.22
  83.1 13.4 %collective-permute-done.refs_0_.x_ref = bf16[512,1024]{1,0:T(8,128)(2,1)S(1)} collective-permute-done((bf16[512,1024]{1,0:T(8,128)(2,1)S(1)}, bf16[512,1024]{1,0:T(8,128)(2,1)S(1)}, u32[]{:S(2)}, u32[]{:S(2)}) %collective-permute-start) | collective-permute-done | bytes 1048608 | tf_op jit(solution)/shard_map/ppermute | solution.py:224
  96.5 2.8 %peer_forward.1 = (bf16[512,1024]{1,0:T(8,128)(2,1)S(1)}, bf16[512,1024]{1,0:T(8,128)(2,1)S(1)}, bf16[512,1024]{1,0:T(8,128)(2,1)S(1)}, bf16[512,1024]{1,0:T(8,128)(2,1)S(1)}) custom-call(bf16[512,1024]{1,0:T(8,128)(2,1)S(1)} %collective-permute-done.refs_0_.x_ref, f32[1,1024]{1,0:T(1,128)S(1)} %copy-done.8, bf16[1024,1024]{1,0:T(8,128)(2,1)S(1)} %bitcast.16, ...), custom_call_target="tpu_custom_call" | custom-call | flops 2147483648 | bytes 9437184 | tf_op jit(solution)/shard_map/peer_forward/pallas_call | solution.py:209
  99.3 0.0 copy-done.22
  99.3 0.0 copy-start.16
  99.3 1.0 copy-done.16
  100.3 1.0 copy-done.18
  101.3 2.6 %collective-permute-start.3 = (bf16[512,1024]{1,0:T(8,128)(2,1)S(1)}, bf16[512,1024]{1,0:T(8,128)(2,1)S(1)}, u32[]{:S(2)}, u32[]{:S(2)}) collective-permute-start(bf16[512,1024]{1,0:T(8,128)(2,1)S(1)} %get-tuple-element.39.part_ref), channel_id=1, source_target_pairs={{0,1},{1,0},{2,3},{3,2},{4,5},{5,4},{6,7},{7,6},{8,9},{9,8},{10,11... | collective-permute-start | bytes 3145736 | tf_op jit(solution)/shard_map/ppermute | solution.py:224
  103.9 15.1 %collective-permute-done.1.db_ref.refs_7_ = bf16[512,1024]{1,0:T(8,128)(2,1)S(1)} collective-permute-done((bf16[512,1024]{1,0:T(8,128)(2,1)S(1)}, bf16[512,1024]{1,0:T(8,128)(2,1)S(1)}, u32[]{:S(2)}, u32[]{:S(2)}) %collective-permute-start.1) | collective-permute-done | bytes 1048608 | tf_op jit(solution)/shard_map/ppermute | solution.py:224
  119.0 4.6 %peer_backward.1 = (bf16[512,1024]{1,0:T(8,128)(2,1)S(1)}, bf16[528,1024]{1,0:T(8,128)(2,1)}) custom-call(bf16[512,1024]{1,0:T(8,128)(2,1)S(1)} %collective-permute-done.refs_0_.x_ref, bf16[512,1024]{1,0:T(8,128)(2,1)S(1)} %collective-permute-done.1.db_ref.refs_7_, bf16[512,1024]{1,0:T(8,128)(2,1)S(1)} %get-tuple-element.38.slope_ref, ...), custom_call_target="tpu_custom_call" | custom-call | flops 2147483648 | bytes 9437184 | tf_op jit(solution)/shard_map/peer_backward/pallas_call | solution.py:209
  123.6 2.6 %collective-permute-start.2 = (bf16[528,1024]{1,0:T(8,128)(2,1)}, bf16[528,1024]{1,0:T(8,128)(2,1)}, u32[]{:S(2)}, u32[]{:S(2)}) collective-permute-start(bf16[528,1024]{1,0:T(8,128)(2,1)} %get-tuple-element.40.refs_1_), channel_id=1, source_target_pairs={{0,1},{1,0},{2,3},{3,2},{4,5},{5,4},{6,7},{7,6},{8,9},{9,8},{10,11... | collective-permute-start | bytes 3244040 | tf_op jit(solution)/shard_map/ppermute | solution.py:224
  126.2 15.2 %collective-permute-done.3.recv_ref = bf16[512,1024]{1,0:T(8,128)(2,1)S(1)} collective-permute-done((bf16[512,1024]{1,0:T(8,128)(2,1)S(1)}, bf16[512,1024]{1,0:T(8,128)(2,1)S(1)}, u32[]{:S(2)}, u32[]{:S(2)}) %collective-permute-start.3) | collective-permute-done | bytes 1048608 | tf_op jit(solution)/shard_map/ppermute | solution.py:224
  141.4 0.0 copy-done
  141.4 3.0 %mix.1.refs_8_ = bf16[1024,1024]{1,0:T(8,128)(2,1)} custom-call(bf16[512,1024]{1,0:T(8,128)(2,1)S(1)} %get-tuple-element.32.x_ref, f32[512,1024]{1,0:T(8,128)S(1)} %get-tuple-element.47.part_ref, bf16[512,1024]{1,0:T(8,128)(2,1)S(1)} %collective-permute-done.3.recv_ref, bf16[1,1024]{1,0:T(2,128)(2,1)S(1)} %copy-done.7, ...), custom_call_target="tpu_custom_call" | custom-call | flops 1073741824 | bytes 8388608 | tf_op jit(solution)/shard_map/mix/pallas_call | solution.py:209
  144.4 0.0 copy-done.13
  144.4 7.8 %all-to-all-start.1 = ((bf16[64,16,1024]{2,1,0:T(8,128)(2,1)}), bf16[64,16,1024]{2,1,0:T(8,128)(2,1)}, u32[]{:S(2)}, u32[]{:S(2)}) async-start(bf16[64,16,1024]{2,1,0:T(8,128)(2,1)} %bitcast.4), calls=%async_computation.1 | async-start | bytes 4194304 | tf_op jit(solution)/shard_map/all_to_all | solution.py:228
  152.2 0.0 copy-start.12
  152.2 1.2 copy-done.12
  153.4 1.2 copy-done.14
  154.6 1.2 copy-done.17
  155.9 1.2 copy-done.19
  157.1 1.2 copy-done.21
  158.3 1.2 copy-done.23
  159.5 1.2 copy-done.25
  160.8 6.5 %weight_grads.1 = (f32[1024,1024]{1,0:T(8,128)}, f32[1024,1024]{1,0:T(8,128)}) custom-call(bf16[512,1024]{1,0:T(8,128)(2,1)S(1)} %copy-done.25, bf16[512,1024]{1,0:T(8,128)(2,1)S(1)} %copy-done.14, bf16[512,1024]{1,0:T(8,128)(2,1)S(1)} %copy-done.21, bf16[512,1024]{1,0:T(8,128)(2,1)S(1)} %copy-done.17, bf16[512,1024]{1,0:T(8,128)(2,1)S(1)} %copy-done.23, ...), custom_call_target="tpu_custom_call" | custom-call | flops 999999995904 | bytes 16777216 | tf_op jit(solution)/shard_map/weight_grads/pallas_call | solution.py:209
  167.3 14.3 %collective-permute-done.2.refs_2_ = bf16[528,1024]{1,0:T(8,128)(2,1)} collective-permute-done((bf16[528,1024]{1,0:T(8,128)(2,1)}, bf16[528,1024]{1,0:T(8,128)(2,1)}, u32[]{:S(2)}, u32[]{:S(2)}) %collective-permute-start.2) | collective-permute-done | bytes 1081376 | tf_op jit(solution)/shard_map/ppermute | solution.py:224
  181.6 0.0 copy-done.1
  181.6 2.2 copy-done.2
  183.8 2.9 %add_back.1 = (bf16[1024,1024]{1,0:T(8,128)(2,1)S(1)}, f32[2,1024]{1,0:T(2,128)S(1)}) custom-call(f32[512,1024]{1,0:T(8,128)S(1)} %get-tuple-element.36.refs_0_, bf16[528,1024]{1,0:T(8,128)(2,1)} %get-tuple-element.40.refs_1_, bf16[528,1024]{1,0:T(8,128)(2,1)} %collective-permute-done.2.refs_2_, f32[1024,128]{1,0:T(8,128)S(1)} %copy-done.1, ...), custom_call_target="tpu_custom_call" | custom-call | flops 1073741824 | bytes 5242880 | tf_op jit(solution)/shard_map/add_back/pallas_call | solution.py:209
  186.6 0.0 copy-start.3
  186.6 1.4 copy-done.3
  188.0 0.0 all-to-all-done.1
  188.0 7.6 %all-to-all-start.2 = ((bf16[64,16,1024]{2,1,0:T(8,128)(2,1)}), bf16[64,16,1024]{2,1,0:T(8,128)(2,1)S(1)}, u32[]{:S(2)}, u32[]{:S(2)}) async-start(bf16[64,16,1024]{2,1,0:T(8,128)(2,1)} %bitcast.14), calls=%async_computation.2 | async-start | bytes 4194304 | tf_op jit(solution)/shard_map/all_to_all | solution.py:228
  195.6 0.6 fusion
  196.2 3.8 %unpack.2.refs_2_ = bf16[512,1024]{1,0:T(8,128)(2,1)} custom-call(s32[1,512]{1,0:T(1,128)S(1)} %get-tuple-element.30.slot_ref.refs_0_, bf16[1024,1024]{1,0:T(8,128)(2,1)} %bitcast.5.buf_ref), custom_call_target="tpu_custom_call" | custom-call | flops 1073741824 | bytes 3145728 | tf_op jit(solution)/shard_map/unpack/pallas_call | solution.py:209
  200.0 24.6 %all-to-all-done.2 = bf16[64,16,1024]{2,1,0:T(8,128)(2,1)S(1)} async-done(((bf16[64,16,1024]{2,1,0:T(8,128)(2,1)}), bf16[64,16,1024]{2,1,0:T(8,128)(2,1)S(1)}, u32[]{:S(2)}, u32[]{:S(2)}) %all-to-all-start.2) | async-done | bytes 2097184 | tf_op jit(solution)/shard_map/all_to_all | solution.py:228
  224.6 1.2 copy-done.6
  225.8 2.3 unpack.3
  (13 shorter events, 0.0 us)
Async XLA Ops:
  0.6 1.2 copy-start.9
  1.9 1.2 copy-start.10
  3.1 0.7 copy-start.15
  68.6 4.5 %copy-start.7 = (bf16[1,1024]{1,0:T(2,128)(2,1)S(1)}, bf16[1,1024]{1,0:T(2,128)(2,1)}, u32[]{:S(2)}) copy-start(bf16[1,1024]{1,0:T(2,128)(2,1)} %router_ref.7) | copy-start | bytes 6148
  70.3 71.1 %copy-start = (f32[1024,128]{1,0:T(8,128)}, f32[1024,128]{1,0:T(8,128)S(1)}, u32[]{:S(2)}) copy-start(f32[1024,128]{1,0:T(8,128)S(1)} %get-tuple-element.33.pos_ref.refs_3_) | copy-start | bytes 1572868
  70.3 26.2 %collective-permute-start = (bf16[512,1024]{1,0:T(8,128)(2,1)S(1)}, bf16[512,1024]{1,0:T(8,128)(2,1)S(1)}, u32[]{:S(2)}, u32[]{:S(2)}) collective-permute-start(bf16[512,1024]{1,0:T(8,128)(2,1)S(1)} %get-tuple-element.32.x_ref), channel_id=1, source_target_pairs={{0,1},{1,0},{2,3},{3,2},{4,5},{5,4},{6,7},{7,6},{8,9},{9,8},{10,11... | collective-permute-start | bytes 3145736 | tf_op jit(solution)/shard_map/ppermute | solution.py:224
  73.0 2.0 copy-start.4
  73.0 2.2 copy-start.5
  73.0 2.2 copy-start.8
  74.4 6.7 %copy-start.11 = (bf16[512,1024]{1,0:T(8,128)(2,1)}, bf16[512,1024]{1,0:T(8,128)(2,1)S(1)}, u32[]{:S(2)}) copy-start(bf16[512,1024]{1,0:T(8,128)(2,1)S(1)} %get-tuple-element.34.db_ref.refs_6_) | copy-start | bytes 3145732
  74.4 44.5 %collective-permute-start.1 = (bf16[512,1024]{1,0:T(8,128)(2,1)S(1)}, bf16[512,1024]{1,0:T(8,128)(2,1)S(1)}, u32[]{:S(2)}, u32[]{:S(2)}) collective-permute-start(bf16[512,1024]{1,0:T(8,128)(2,1)S(1)} %get-tuple-element.34.db_ref.refs_6_), channel_id=1, source_target_pairs={{0,1},{1,0},{2,3},{3,2},{4,5},{5,4},{6,7},{7,6},{8,9},{9,8},{10,11... | collective-permute-start | bytes 3145736 | tf_op jit(solution)/shard_map/ppermute | solution.py:224
  81.1 1.0 copy-start.20
  82.1 1.0 copy-start.24
  83.1 16.2 %copy-start.22 = (bf16[512,1024]{1,0:T(8,128)(2,1)}, bf16[512,1024]{1,0:T(8,128)(2,1)S(1)}, u32[]{:S(2)}) copy-start(bf16[512,1024]{1,0:T(8,128)(2,1)S(1)} %get-tuple-element.45.refs_4_) | copy-start | bytes 3145732
  99.3 1.0 copy-start.16
  100.3 1.0 copy-start.18
  101.3 40.2 %collective-permute-start.3 = (bf16[512,1024]{1,0:T(8,128)(2,1)S(1)}, bf16[512,1024]{1,0:T(8,128)(2,1)S(1)}, u32[]{:S(2)}, u32[]{:S(2)}) collective-permute-start(bf16[512,1024]{1,0:T(8,128)(2,1)S(1)} %get-tuple-element.39.part_ref), channel_id=1, source_target_pairs={{0,1},{1,0},{2,3},{3,2},{4,5},{5,4},{6,7},{7,6},{8,9},{9,8},{10,11... | collective-permute-start | bytes 3145736 | tf_op jit(solution)/shard_map/ppermute | solution.py:224
  123.6 20.8 %copy-start.13 = (bf16[512,1024]{1,0:T(8,128)(2,1)}, bf16[512,1024]{1,0:T(8,128)(2,1)S(1)}, u32[]{:S(2)}) copy-start(bf16[512,1024]{1,0:T(8,128)(2,1)S(1)} %get-tuple-element.42.refs_1_) | copy-start | bytes 3145732
  123.6 58.0 %collective-permute-start.2 = (bf16[528,1024]{1,0:T(8,128)(2,1)}, bf16[528,1024]{1,0:T(8,128)(2,1)}, u32[]{:S(2)}, u32[]{:S(2)}) collective-permute-start(bf16[528,1024]{1,0:T(8,128)(2,1)} %get-tuple-element.40.refs_1_), channel_id=1, source_target_pairs={{0,1},{1,0},{2,3},{3,2},{4,5},{5,4},{6,7},{7,6},{8,9},{9,8},{10,11... | collective-permute-start | bytes 3244040 | tf_op jit(solution)/shard_map/ppermute | solution.py:224
  144.4 43.6 %all-to-all-start.1 = ((bf16[64,16,1024]{2,1,0:T(8,128)(2,1)}), bf16[64,16,1024]{2,1,0:T(8,128)(2,1)}, u32[]{:S(2)}, u32[]{:S(2)}) async-start(bf16[64,16,1024]{2,1,0:T(8,128)(2,1)} %bitcast.4), calls=%async_computation.1 | async-start | bytes 4194304 | tf_op jit(solution)/shard_map/all_to_all | solution.py:228
  152.2 1.2 copy-start.12
  153.4 1.2 copy-start.14
  154.6 1.2 copy-start.17
  155.8 1.2 copy-start.19
  157.1 1.2 copy-start.21
  158.3 1.2 copy-start.23
  159.5 1.2 copy-start.25
  160.8 20.8 %copy-start.1 = (f32[1024,128]{1,0:T(8,128)S(1)}, f32[1024,128]{1,0:T(8,128)}, u32[]{:S(2)}) copy-start(f32[1024,128]{1,0:T(8,128)} %copy-done) | copy-start | bytes 1572868
  181.6 2.2 copy-start.2
  186.6 1.4 copy-start.3
  188.0 36.6 %all-to-all-start.2 = ((bf16[64,16,1024]{2,1,0:T(8,128)(2,1)}), bf16[64,16,1024]{2,1,0:T(8,128)(2,1)S(1)}, u32[]{:S(2)}, u32[]{:S(2)}) async-start(bf16[64,16,1024]{2,1,0:T(8,128)(2,1)} %bitcast.14), calls=%async_computation.2 | async-start | bytes 4194304 | tf_op jit(solution)/shard_map/all_to_all | solution.py:228
  224.6 1.2 copy-start.6

commit v3 on v2

--- a/solution.py
+++ b/solution.py
@@ -14,7 +14,7 @@
 F32 = jnp.float32
 MIB = 1024 * 1024
 TAIL = 16
-GF = 10**12
+LONG = 10**12
 
 
 def dot(left, right, dims):
@@ -44,6 +44,25 @@
     half = 0.5 + 0.5 * wave
     slope = half + pre * (0.5 - 0.5 * wave * wave) * (root + root * 0.134145 * square)
     return pre * half, slope
+
+
+def copies(pairs, sems, first=0):
+    return [pltpu.make_async_copy(src, dst, sems.at[first + i]) for i, (src, dst) in enumerate(pairs)]
+
+
+def pieces(src, dst, count):
+    step = src.shape[0] // count
+    return [(src.at[pl.ds(i * step, step)], dst.at[pl.ds(i * step, step)]) for i in range(count)]
+
+
+def start(group):
+    for copy in group:
+        copy.start()
+
+
+def wait(group):
+    for copy in group:
+        copy.wait()
 
 
 def pack_kernel(experts, cap, assign_ref, x_ref, dy_ref, out_ref, slot_ref):
@@ -141,7 +160,7 @@
 
 def peer_backward_kernel(
     x_ref, db_ref, slope_ref, part_ref, small_ref, gain_ref, router_ref, win_ref, wout_ref,
-    dpre_ref, back_ref,
+    dpre_ref, back_ref, tail_ref,
 ):
     tok = x_ref.shape[0]
     back, gain_part, router_part = backward(
@@ -157,9 +176,11 @@
     pad = jnp.zeros((TAIL - 6, small.shape[1]), F32)
     coded = jnp.concatenate([high.astype(F32), middle.astype(F32), low.astype(F32), pad], 0)
     back_ref[tok:, :] = coded.astype(BF)
-
-
-def grads_kernel(dpo, dpp, no, np_, ho, hp, bo, bp, gin_ref, gout_ref):
+    tail_ref[...] = coded.astype(BF)
+
+
+def grads_kernel(dpo, dpp, no, np_, ho, hp, bo, bp, gin_ref, gout_ref, done_ref):
+    done_ref[...] = jnp.zeros_like(done_ref)
     first = ((0,), (0,))
     gin_ref[...] = dot(dpo[...], no[...], first) + dot(dpp[...], np_[...], first)
     gout_ref[...] = dot(ho[...], bo[...], first) + dot(hp[...], bp[...], first)
@@ -170,7 +191,8 @@
     out_ref[...] = dot(place, rows, ((1,), (0,))).astype(BF)
 
 
-def mix_kernel(x_ref, part_ref, recv_ref, router_ref, pos_ref, out_ref):
+def mix_kernel(x_ref, part_ref, recv_ref, router_ref, pos_ref, out_ref, done_ref):
+    done_ref[...] = jnp.zeros_like(done_ref)
     xf = x_ref[...].astype(F32)
     gate = gate_of(xf, router_ref[...].astype(F32))
     rows = (xf + gate * (part_ref[...] + recv_ref[...].astype(F32))).astype(BF)
@@ -178,21 +200,49 @@
 
 
 def decode(ref, tok):
-    coded = ref[tok:, :].astype(F32)
+    coded = ref[tok : tok + TAIL, :].astype(F32)
     return coded[0:2] + coded[2:4] + coded[4:6]
 
 
-def add_kernel(own_ref, sent_ref, recv_ref, pos_ref, out_ref, small_ref):
-    tok = own_ref.shape[0]
-    rows = (own_ref[...] + recv_ref[:tok, :].astype(F32)).astype(BF)
-    spread(pos_ref, rows, out_ref)
-    small_ref[...] = decode(sent_ref, tok) + decode(recv_ref, tok)
-
-
-def unpack_kernel(slot_ref, buf_ref, out_ref):
+def add_kernel(own_ref, tail_ref, recv_ref, pos_ref, out_ref, small_ref, recv, out, sems):
+    tok, slots = own_ref.shape[0], out.shape[0]
+    loads = copies(pieces(recv_ref, recv, 3), sems)
+    start(loads)
+    place = mask(iota((slots, tok), 1).astype(F32) == pos_ref[:, :1])
+    wait(loads)
+    rows = (own_ref[...] + recv[:tok, :].astype(F32)).astype(BF)
+    step = slots // 2
+    stores = []
+    for part in range(2):
+        at = pl.ds(part * step, step)
+        out[at, :] = dot(place[part * step : (part + 1) * step], rows, ((1,), (0,))).astype(BF)
+        group = copies(pieces(out.at[at], out_ref.at[at], 2), sems, 3 + 2 * part)
+        start(group)
+        stores += group
+    small_ref[...] = decode(tail_ref, 0) + decode(recv, tok)
+    wait(stores)
+
+
+def unpack_kernel(slot_ref, buf_ref, out_ref, place_ref):
     slots, tok = buf_ref.shape[0], out_ref.shape[0]
-    place = mask(iota((slots, tok), 0) == slot_ref[...])
-    out_ref[...] = dot(place, buf_ref[...], ((0,), (0,))).astype(BF)
+    place = mask(iota((tok, slots), 1) == jnp.broadcast_to(slot_ref[...], (128, tok)).T[:, :1])
+    place_ref[...] = place
+    out_ref[...] = dot(place, buf_ref[...], ((1,), (0,))).astype(BF)
+
+
+def unpack_last_kernel(place_ref, buf_ref, out_ref, buf, out, sems):
+    loads = copies(pieces(buf_ref, buf, 4), sems)
+    start(loads)
+    wait(loads)
+    step = out.shape[0] // 2
+    stores = []
+    for part in range(2):
+        at = pl.ds(part * step, step)
+        out[at, :] = dot(place_ref[at, :], buf[...], ((1,), (0,))).astype(BF)
+        group = copies(pieces(out.at[at], out_ref.at[at], 2), sems, 4 + 2 * part)
+        start(group)
+        stores += group
+    wait(stores)
 
 
 def call(kernel, name, out_shape, flops, moved, inputs, after=None, vmem=32, **kw):
@@ -241,6 +291,8 @@
     hid_bf = shape((tok, hidden), BF)
     slots_bf = shape((slots, width), BF)
 
+    outer = pl.BlockSpec(memory_space=pltpu.HBM)
+    inside = pl.BlockSpec(memory_space=pltpu.VMEM)
     packed, slot = call(
         functools.partial(pack_kernel, experts, cap), "pack",
         (shape((experts, 2 * cap, width), BF), shape((1, tok), jnp.int32)),
@@ -265,34 +317,53 @@
         2 * mm, 9 * MIB, (x_peer, gain, win, wout), small_o,
     )
     part_recv = swap(part_p)
-    dpre_p, back_p = call(
-        peer_backward_kernel, "peer_backward", (hid_bf, shape((tok + TAIL, width), BF)),
+    dpre_p, back_p, tail = call(
+        peer_backward_kernel, "peer_backward", (hid_bf, shape((tok + TAIL, width), BF), shape((TAIL, width), BF)),
         2 * mm, 9 * MIB, (x_peer, db_peer, slope_p, part_p, small_o, gain, router, win, wout),
     )
     back_recv = swap(back_p)
-    y_pack = call(
-        mix_kernel, "mix", slots_bf, place_cost, 8 * MIB, (x_own, part_o, part_recv, router, pos)
+    y_pack, mix_done = call(
+        mix_kernel, "mix", (slots_bf, shape((8, 128), F32)), place_cost, 8 * MIB, (x_own, part_o, part_recv, router, pos)
     )
     half = hidden // 2
     left = pl.BlockSpec((tok, half), lambda i: (0, i))
     right = pl.BlockSpec((tok, width), lambda i: (0, 0))
     grad = pl.BlockSpec((half, width), lambda i: (i, 0))
-    gin, gout = call(
-        grads_kernel, "weight_grads", (shape((hidden, width), F32), shape((hidden, width), F32)),
-        GF, 16 * MIB, (dpre_o, dpre_p, normed_o, normed_p, hid_o, hid_p, db_own, db_peer), y_pack,
+    token = shape((8, 128), F32)
+    gin, gout, grads_done = call(
+        grads_kernel, "weight_grads", (shape((hidden, width), F32), shape((hidden, width), F32), token),
+        LONG, 16 * MIB, (dpre_o, dpre_p, normed_o, normed_p, hid_o, hid_p, db_own, db_peer), mix_done,
         grid=(2,),
         in_specs=[left, left, right, right, left, left, right, right],
-        out_specs=(grad, grad),
+        out_specs=(grad, grad, pl.BlockSpec((8, 128), lambda i: (0, 0))),
     )
     y_buf = exchange(y_pack.reshape(experts, cap, width), experts).reshape(slots, width)
     back_pack, small = call(
         add_kernel, "add_back", (slots_bf, shape((2, width), F32)), place_cost, 5 * MIB,
-        (back_o, back_p, back_recv, pos), gin,
+        (back_o, tail, back_recv, pos), grads_done, 24,
+        in_specs=[inside, inside, outer, inside],
+        out_specs=(outer, inside),
+        scratch_shapes=[
+            pltpu.VMEM((tok + TAIL, width), BF),
+            pltpu.VMEM((slots, width), BF),
+            pltpu.SemaphoreType.DMA((7,)),
+        ],
     )
     back_pack, y_buf = lax.optimization_barrier((back_pack, y_buf))
     back_buf = exchange(back_pack.reshape(experts, cap, width), experts).reshape(slots, width)
-    mixed = call(unpack_kernel, "unpack", rows_bf, place_cost, 3 * MIB, (slot, y_buf))
-    input_grad = call(unpack_kernel, "unpack", rows_bf, place_cost, 3 * MIB, (slot, back_buf), mixed)
+    mixed, place = call(
+        unpack_kernel, "unpack", (rows_bf, shape((tok, slots), BF)), place_cost, 4 * MIB, (slot, y_buf)
+    )
+    input_grad = call(
+        unpack_last_kernel, "unpack_last", rows_bf, place_cost, 4 * MIB, (place, back_buf), None, 40,
+        in_specs=[inside, outer],
+        out_specs=outer,
+        scratch_shapes=[
+            pltpu.VMEM((slots, width), BF),
+            pltpu.VMEM((tok, width), BF),
+            pltpu.SemaphoreType.DMA((8,)),
+        ],
+    )
     return (mixed[None], input_grad[None], gin[None], gout[None], small[:1], small[1:])
 
 

time: 229 us -> 227 us (level)
  local copies, waits for them, and re-layouts: 21.2 us -> 11.5 us
  waiting for transfers between devices: 82.6 us -> 90 us
    unnamed x52 -> x44, local copies, waits for them, and re-layouts: 20.6 us -> 10.9 us
    ppermute x4, waiting for transfers between devices: 58 us -> 64.1 us  [swap(): return lax.ppermute(values, 'dp', SWAP)]
  transfers between devices with their start and end apart: 6 -> 6, of which waited for: 5 -> 6; matrix products, arithmetic and copies ran while one was open for 0% -> 0% of each run, Pallas kernels for 14% -> 14%
where the time goes in v3:
time: 227 us; the launch traced here: 226 us
  waiting for transfers between devices  90 us (40%)
  blocking collectives  62.1 us (27%)
  Pallas kernels  38 us (17%)
  starting transfers between devices  23.5 us (10%)
  local copies, waits for them, and re-layouts  11.5 us (5%)
    ppermute x4, waiting for transfers between devices, swap(): return lax.ppermute(values, 'dp', SWAP)  64.1 us
    all_to_all x1, blocking collectives, exchange(): lax.all_to_all(buffer, 'expert', split_axis=0, concat_axis=0, tiled=True)  62.1 us
    pallas_call x11, Pallas kernels, call(): pl.pallas_call(kernel, name=name, out_shape=out_shape, compiler_params=pl...  38 us
    all_to_all x2, waiting for transfers between devices, exchange(): lax.all_to_all(buffer, 'expert', split_axis=0, concat_axis=0, tiled=True)  25.9 us
    all_to_all x2, starting transfers between devices, exchange(): lax.all_to_all(buffer, 'expert', split_axis=0, concat_axis=0, tiled=True)  14.9 us
    unnamed x44, local copies, waits for them, and re-layouts  10.9 us
    ppermute x4, starting transfers between devices, swap(): return lax.ppermute(values, 'dp', SWAP)  8.63 us
  transfers between devices with their start and end apart: 6, of which 6 were waited for; matrix products, arithmetic and copies ran while one was open for 0% of the time, Pallas kernels for 14%

profile of v3, /device:TPU:1, one launch (start us, length us, event | category | flops | bytes accessed | tf_op | source)
XLA Modules:
  0.0 226.1 jit_solution(9346556991120897292)
XLA Ops:
  0.6 0.0 copy-start.7
  0.6 1.2 copy-done.7
  1.9 0.0 copy-start.8
  1.9 1.2 copy-done.8
  3.1 0.0 copy-start.9
  3.1 0.7 copy-done.9
  3.8 2.7 %pack.1 = (bf16[64,32,1024]{2,1,0:T(8,128)(2,1)S(1)}, s32[1,512]{1,0:T(1,128)S(1)}) custom-call(s32[1,512]{1,0:T(1,128)S(1)} %copy-done.9, bf16[512,1024]{1,0:T(8,128)(2,1)S(1)} %bitcast.20, bf16[512,1024]{1,0:T(8,128)(2,1)S(1)} %bitcast.21), custom_call_target="tpu_custom_call" | custom-call | flops 2147483648 | bytes 6291456 | tf_op jit(solution)/shard_map/pack/pallas_call | solution.py:259
  6.4 62.1 %all_to_all.15.buf_ref = bf16[64,32,1024]{2,1,0:T(8,128)(2,1)S(1)} all-to-all(bf16[64,32,1024]{2,1,0:T(8,128)(2,1)S(1)} %get-tuple-element.37), channel_id=1, replica_groups=mesh['expert'=64,'dp'=2] {'expert'}, dimensions={0} | all-to-all | bytes 8388608 | tf_op jit(solution)/shard_map/all_to_all | solution.py:278
  68.6 0.0 copy-start.5
  68.6 1.8 compact_x.1
  70.3 0.0 copy-start.3
  70.3 2.7 %collective-permute-start = (bf16[512,1024]{1,0:T(8,128)(2,1)S(1)}, bf16[512,1024]{1,0:T(8,128)(2,1)S(1)}, u32[]{:S(2)}, u32[]{:S(2)}) collective-permute-start(bf16[512,1024]{1,0:T(8,128)(2,1)S(1)} %get-tuple-element.38.x_ref), channel_id=1, source_target_pairs={{0,1},{1,0},{2,3},{3,2},{4,5},{5,4},{6,7},{7,6},{8,9},{9,8},{10,11... | collective-permute-start | bytes 3145736 | tf_op jit(solution)/shard_map/ppermute | solution.py:274
  73.0 0.0 copy-done.5
  73.0 0.0 copy-start.1
  73.0 0.0 copy-start.2
  73.0 0.0 copy-start.6
  73.1 1.4 compact_dy.1
  74.4 0.6 collective-permute-start.1
  75.0 0.0 copy-done.1
  75.0 0.2 copy-done.2
  75.3 0.0 copy-done.6
  75.3 5.9 %own.1 = (bf16[512,1024]{1,0:T(8,128)(2,1)S(1)}, bf16[512,1024]{1,0:T(8,128)(2,1)S(1)}, bf16[512,1024]{1,0:T(8,128)(2,1)S(1)}, f32[512,1024]{1,0:T(8,128)S(1)}, ...) custom-call(bf16[512,1024]{1,0:T(8,128)(2,1)S(1)} %get-tuple-element.38.x_ref, ...), custom_call_target="tpu_custom_call" | custom-call | flops 4294967296 | bytes 14680064 | tf_op jit(solution)/shard_map/own/pallas_call | solution.py:259
  81.1 0.0 copy-start.10
  81.2 0.0 copy-start.16
  81.2 0.0 copy-start.18
  81.2 0.0 copy-start.20
  81.2 15.3 %collective-permute-done.refs_0_.x_ref = bf16[512,1024]{1,0:T(8,128)(2,1)S(1)} collective-permute-done((bf16[512,1024]{1,0:T(8,128)(2,1)S(1)}, bf16[512,1024]{1,0:T(8,128)(2,1)S(1)}, u32[]{:S(2)}, u32[]{:S(2)}) %collective-permute-start) | collective-permute-done | bytes 1048608 | tf_op jit(solution)/shard_map/ppermute | solution.py:274
  96.5 2.8 %peer_forward.1 = (bf16[512,1024]{1,0:T(8,128)(2,1)S(1)}, bf16[512,1024]{1,0:T(8,128)(2,1)S(1)}, bf16[512,1024]{1,0:T(8,128)(2,1)S(1)}, bf16[512,1024]{1,0:T(8,128)(2,1)S(1)}) custom-call(bf16[512,1024]{1,0:T(8,128)(2,1)S(1)} %collective-permute-done.refs_0_.x_ref, f32[1,1024]{1,0:T(1,128)S(1)} %copy-done.6, bf16[1024,1024]{1,0:T(8,128)(2,1)S(1)} %bitcast.15, ...), custom_call_target="tpu_custom_call" | custom-call | flops 2147483648 | bytes 9437184 | tf_op jit(solution)/shard_map/peer_forward/pallas_call | solution.py:259
  99.3 0.0 copy-done.10
  99.3 0.0 copy-done.16
  99.3 0.0 copy-done.18
  99.4 0.0 copy-done.20
  99.4 0.0 copy-start.12
  99.4 0.0 copy-start.14
  99.4 2.7 %collective-permute-start.3 = (bf16[512,1024]{1,0:T(8,128)(2,1)S(1)}, bf16[512,1024]{1,0:T(8,128)(2,1)S(1)}, u32[]{:S(2)}, u32[]{:S(2)}) collective-permute-start(bf16[512,1024]{1,0:T(8,128)(2,1)S(1)} %get-tuple-element.45.part_ref), channel_id=1, source_target_pairs={{0,1},{1,0},{2,3},{3,2},{4,5},{5,4},{6,7},{7,6},{8,9},{9,8},{10,11... | collective-permute-start | bytes 3145736 | tf_op jit(solution)/shard_map/ppermute | solution.py:274
  102.1 16.9 %collective-permute-done.1.db_ref.refs_7_ = bf16[512,1024]{1,0:T(8,128)(2,1)S(1)} collective-permute-done((bf16[512,1024]{1,0:T(8,128)(2,1)S(1)}, bf16[512,1024]{1,0:T(8,128)(2,1)S(1)}, u32[]{:S(2)}, u32[]{:S(2)}) %collective-permute-start.1) | collective-permute-done | bytes 1048608 | tf_op jit(solution)/shard_map/ppermute | solution.py:274
  119.0 4.7 %peer_backward.1 = (bf16[512,1024]{1,0:T(8,128)(2,1)S(1)}, bf16[528,1024]{1,0:T(8,128)(2,1)}, bf16[16,1024]{1,0:T(8,128)(2,1)S(1)}) custom-call(bf16[512,1024]{1,0:T(8,128)(2,1)S(1)} %collective-permute-done.refs_0_.x_ref, bf16[512,1024]{1,0:T(8,128)(2,1)S(1)} %collective-permute-done.1.db_ref.refs_7_, bf16[512,1024]{1,0:T(8,128)(2,1)S(1)} %get-tuple-element.44.slope_ref, ...), custom_call_target="tpu_custom_call" | custom-call | flops 2147483648 | bytes 9437184 | tf_op jit(solution)/shard_map/peer_backward/pallas_call | solution.py:259
  123.7 0.0 copy-done.12
  123.7 0.0 copy-done.14
  123.7 2.6 %collective-permute-start.2 = (bf16[528,1024]{1,0:T(8,128)(2,1)}, bf16[528,1024]{1,0:T(8,128)(2,1)}, u32[]{:S(2)}, u32[]{:S(2)}) collective-permute-start(bf16[528,1024]{1,0:T(8,128)(2,1)} %get-tuple-element.47), channel_id=1, source_target_pairs={{0,1},{1,0},{2,3},{3,2},{4,5},{5,4},{6,7},{7,6},{8,9},{9,8},{10,11... | collective-permute-start | bytes 3244040 | tf_op jit(solution)/shard_map/ppermute | solution.py:274
  126.3 15.2 %collective-permute-done.3.recv_ref = bf16[512,1024]{1,0:T(8,128)(2,1)S(1)} collective-permute-done((bf16[512,1024]{1,0:T(8,128)(2,1)S(1)}, bf16[512,1024]{1,0:T(8,128)(2,1)S(1)}, u32[]{:S(2)}, u32[]{:S(2)}) %collective-permute-start.3) | collective-permute-done | bytes 1048608 | tf_op jit(solution)/shard_map/ppermute | solution.py:274
  141.4 0.0 copy-done.3
  141.4 3.0 %mix.1 = (bf16[1024,1024]{1,0:T(8,128)(2,1)}, f32[8,128]{1,0:T(8,128)S(1)}) custom-call(bf16[512,1024]{1,0:T(8,128)(2,1)S(1)} %get-tuple-element.38.x_ref, f32[512,1024]{1,0:T(8,128)S(1)} %get-tuple-element.54.part_ref, bf16[512,1024]{1,0:T(8,128)(2,1)S(1)} %collective-permute-done.3.recv_ref, bf16[1,1024]{1,0:T(2,128)(2,1)S(1)} %copy-done.5, ...), custom_call_target="tpu_custom_call" | custom-call | flops 1073741824 | bytes 8388608 | tf_op jit(solution)/shard_map/mix/pallas_call | solution.py:259
  144.5 7.7 %all-to-all-start.1 = ((bf16[64,16,1024]{2,1,0:T(8,128)(2,1)}), bf16[64,16,1024]{2,1,0:T(8,128)(2,1)}, u32[]{:S(2)}, u32[]{:S(2)}) async-start(bf16[64,16,1024]{2,1,0:T(8,128)(2,1)} %bitcast.4), calls=%async_computation.1 | async-start | bytes 4194304 | tf_op jit(solution)/shard_map/all_to_all | solution.py:278
  152.2 0.0 copy-start.13
  152.2 1.2 copy-done.13
  153.4 0.0 copy-start.15
  153.4 1.2 copy-done.15
  154.7 1.2 copy-done.17
  155.9 1.2 copy-done.19
  157.1 1.2 copy-done.21
  158.3 6.5 %weight_grads.1 = (f32[1024,1024]{1,0:T(8,128)}, f32[1024,1024]{1,0:T(8,128)}, f32[8,128]{1,0:T(8,128)S(1)}) custom-call(bf16[512,1024]{1,0:T(8,128)(2,1)S(1)} %copy-done.21, bf16[512,1024]{1,0:T(8,128)(2,1)S(1)} %get-tuple-element.49.refs_1_, bf16[512,1024]{1,0:T(8,128)(2,1)S(1)} %copy-done.17, bf16[512,1024]{1,0:T(8,128)(2,1)S(1)} %copy-done.13, ...), custom_call_target="tpu_custom_call" | custom-call | flops 999999995904 | bytes 16777216 | tf_op jit(solution)/shard_map/weight_grads/pallas_call | solution.py:259
  164.9 16.7 %collective-permute-done.2.refs_2_ = bf16[528,1024]{1,0:T(8,128)(2,1)} collective-permute-done((bf16[528,1024]{1,0:T(8,128)(2,1)}, bf16[528,1024]{1,0:T(8,128)(2,1)}, u32[]{:S(2)}, u32[]{:S(2)}) %collective-permute-start.2) | collective-permute-done | bytes 1081376 | tf_op jit(solution)/shard_map/ppermute | solution.py:274
  181.6 0.0 copy-done.4
  181.6 0.0 copy-done.11
  181.6 2.9 %add_back.1 = (bf16[1024,1024]{1,0:T(8,128)(2,1)S(1)}, f32[2,1024]{1,0:T(2,128)S(1)}) custom-call(f32[512,1024]{1,0:T(8,128)S(1)} %copy-done.11, bf16[16,1024]{1,0:T(8,128)(2,1)S(1)} %get-tuple-element.46.refs_1_, bf16[528,1024]{1,0:T(8,128)(2,1)} %collective-permute-done.2.refs_2_, f32[1024,128]{1,0:T(8,128)S(1)} %copy-done.4, ...), custom_call_target="tpu_custom_call" | custom-call | flops 1073741824 | bytes 5242880 | tf_op jit(solution)/shard_map/add_back/pallas_call | solution.py:259
  184.5 0.0 copy-start
  184.5 1.3 copy-done
  185.8 1.7 all-to-all-done.1
  187.5 7.2 %all-to-all-start.2 = ((bf16[64,16,1024]{2,1,0:T(8,128)(2,1)}), bf16[64,16,1024]{2,1,0:T(8,128)(2,1)S(1)}, u32[]{:S(2)}, u32[]{:S(2)}) async-start(bf16[64,16,1024]{2,1,0:T(8,128)(2,1)} %bitcast.13), calls=%async_computation.2 | async-start | bytes 4194304 | tf_op jit(solution)/shard_map/all_to_all | solution.py:278
  194.7 0.6 fusion
  195.3 4.2 %unpack.1 = (bf16[512,1024]{1,0:T(8,128)(2,1)}, bf16[512,1024]{1,0:T(8,128)(2,1)S(1)}) custom-call(s32[1,512]{1,0:T(1,128)S(1)} %get-tuple-element.36.slot_ref, bf16[1024,1024]{1,0:T(8,128)(2,1)} %bitcast.5.buf_ref), custom_call_target="tpu_custom_call" | custom-call | flops 1073741824 | bytes 4194304 | tf_op jit(solution)/shard_map/unpack/pallas_call | solution.py:259
  199.4 24.2 %all-to-all-done.2 = bf16[64,16,1024]{2,1,0:T(8,128)(2,1)S(1)} async-done(((bf16[64,16,1024]{2,1,0:T(8,128)(2,1)}), bf16[64,16,1024]{2,1,0:T(8,128)(2,1)S(1)}, u32[]{:S(2)}, u32[]{:S(2)}) %all-to-all-start.2) | async-done | bytes 2097184 | tf_op jit(solution)/shard_map/all_to_all | solution.py:278
  223.7 2.3 unpack_last.1
  (5 shorter events, 0.0 us)
Async XLA Ops:
  0.6 1.2 copy-start.7
  1.9 1.2 copy-start.8
  3.1 0.7 copy-start.9
  68.6 4.5 %copy-start.5 = (bf16[1,1024]{1,0:T(2,128)(2,1)S(1)}, bf16[1,1024]{1,0:T(2,128)(2,1)}, u32[]{:S(2)}) copy-start(bf16[1,1024]{1,0:T(2,128)(2,1)} %router_ref.7) | copy-start | bytes 6148
  70.3 71.1 %copy-start.3 = (f32[1024,128]{1,0:T(8,128)}, f32[1024,128]{1,0:T(8,128)S(1)}, u32[]{:S(2)}) copy-start(f32[1024,128]{1,0:T(8,128)S(1)} %get-tuple-element.39.pos_ref.refs_3_) | copy-start | bytes 1572868
  70.3 26.2 %collective-permute-start = (bf16[512,1024]{1,0:T(8,128)(2,1)S(1)}, bf16[512,1024]{1,0:T(8,128)(2,1)S(1)}, u32[]{:S(2)}, u32[]{:S(2)}) collective-permute-start(bf16[512,1024]{1,0:T(8,128)(2,1)S(1)} %get-tuple-element.38.x_ref), channel_id=1, source_target_pairs={{0,1},{1,0},{2,3},{3,2},{4,5},{5,4},{6,7},{7,6},{8,9},{9,8},{10,11... | collective-permute-start | bytes 3145736 | tf_op jit(solution)/shard_map/ppermute | solution.py:274
  73.0 2.0 copy-start.1
  73.0 2.2 copy-start.2
  73.0 2.2 copy-start.6
  74.4 44.5 %collective-permute-start.1 = (bf16[512,1024]{1,0:T(8,128)(2,1)S(1)}, bf16[512,1024]{1,0:T(8,128)(2,1)S(1)}, u32[]{:S(2)}, u32[]{:S(2)}) collective-permute-start(bf16[512,1024]{1,0:T(8,128)(2,1)S(1)} %get-tuple-element.40.db_ref.refs_6_), channel_id=1, source_target_pairs={{0,1},{1,0},{2,3},{3,2},{4,5},{5,4},{6,7},{7,6},{8,9},{9,8},{10,11... | collective-permute-start | bytes 3145736 | tf_op jit(solution)/shard_map/ppermute | solution.py:274
  81.1 18.2 %copy-start.10 = (f32[512,1024]{1,0:T(8,128)}, f32[512,1024]{1,0:T(8,128)S(1)}, u32[]{:S(2)}) copy-start(f32[512,1024]{1,0:T(8,128)S(1)} %get-tuple-element.42.refs_0_) | copy-start | bytes 6291460
  81.2 18.2 %copy-start.16 = (bf16[512,1024]{1,0:T(8,128)(2,1)}, bf16[512,1024]{1,0:T(8,128)(2,1)S(1)}, u32[]{:S(2)}) copy-start(bf16[512,1024]{1,0:T(8,128)(2,1)S(1)} %get-tuple-element.50.refs_2_) | copy-start | bytes 3145732
  81.2 18.2 %copy-start.18 = (bf16[512,1024]{1,0:T(8,128)(2,1)}, bf16[512,1024]{1,0:T(8,128)(2,1)S(1)}, u32[]{:S(2)}) copy-start(bf16[512,1024]{1,0:T(8,128)(2,1)S(1)} %get-tuple-element.52.refs_4_) | copy-start | bytes 3145732
  81.2 18.2 %copy-start.20 = (bf16[512,1024]{1,0:T(8,128)(2,1)}, bf16[512,1024]{1,0:T(8,128)(2,1)S(1)}, u32[]{:S(2)}) copy-start(bf16[512,1024]{1,0:T(8,128)(2,1)S(1)} %get-tuple-element.48.refs_0_) | copy-start | bytes 3145732
  99.4 24.3 %copy-start.12 = (bf16[512,1024]{1,0:T(8,128)(2,1)}, bf16[512,1024]{1,0:T(8,128)(2,1)S(1)}, u32[]{:S(2)}) copy-start(bf16[512,1024]{1,0:T(8,128)(2,1)S(1)} %get-tuple-element.51.refs_3_) | copy-start | bytes 3145732
  99.4 24.3 %copy-start.14 = (bf16[512,1024]{1,0:T(8,128)(2,1)}, bf16[512,1024]{1,0:T(8,128)(2,1)S(1)}, u32[]{:S(2)}) copy-start(bf16[512,1024]{1,0:T(8,128)(2,1)S(1)} %get-tuple-element.53.refs_5_) | copy-start | bytes 3145732
  99.4 42.1 %collective-permute-start.3 = (bf16[512,1024]{1,0:T(8,128)(2,1)S(1)}, bf16[512,1024]{1,0:T(8,128)(2,1)S(1)}, u32[]{:S(2)}, u32[]{:S(2)}) collective-permute-start(bf16[512,1024]{1,0:T(8,128)(2,1)S(1)} %get-tuple-element.45.part_ref), channel_id=1, source_target_pairs={{0,1},{1,0},{2,3},{3,2},{4,5},{5,4},{6,7},{7,6},{8,9},{9,8},{10,11... | collective-permute-start | bytes 3145736 | tf_op jit(solution)/shard_map/ppermute | solution.py:274
  123.7 57.9 %collective-permute-start.2 = (bf16[528,1024]{1,0:T(8,128)(2,1)}, bf16[528,1024]{1,0:T(8,128)(2,1)}, u32[]{:S(2)}, u32[]{:S(2)}) collective-permute-start(bf16[528,1024]{1,0:T(8,128)(2,1)} %get-tuple-element.47), channel_id=1, source_target_pairs={{0,1},{1,0},{2,3},{3,2},{4,5},{5,4},{6,7},{7,6},{8,9},{9,8},{10,11... | collective-permute-start | bytes 3244040 | tf_op jit(solution)/shard_map/ppermute | solution.py:274
  144.5 43.0 %all-to-all-start.1 = ((bf16[64,16,1024]{2,1,0:T(8,128)(2,1)}), bf16[64,16,1024]{2,1,0:T(8,128)(2,1)}, u32[]{:S(2)}, u32[]{:S(2)}) async-start(bf16[64,16,1024]{2,1,0:T(8,128)(2,1)} %bitcast.4), calls=%async_computation.1 | async-start | bytes 4194304 | tf_op jit(solution)/shard_map/all_to_all | solution.py:278
  152.2 1.2 copy-start.13
  153.4 1.2 copy-start.15
  154.7 1.2 copy-start.17
  155.9 1.2 copy-start.19
  157.1 1.2 copy-start.21
  158.3 23.2 %copy-start.4 = (f32[1024,128]{1,0:T(8,128)S(1)}, f32[1024,128]{1,0:T(8,128)}, u32[]{:S(2)}) copy-start(f32[1024,128]{1,0:T(8,128)} %copy-done.3) | copy-start | bytes 1572868
  158.3 23.2 %copy-start.11 = (f32[512,1024]{1,0:T(8,128)S(1)}, f32[512,1024]{1,0:T(8,128)}, u32[]{:S(2)}) copy-start(f32[512,1024]{1,0:T(8,128)} %copy-done.10) | copy-start | bytes 6291460
  184.5 1.4 copy-start
  187.5 36.2 %all-to-all-start.2 = ((bf16[64,16,1024]{2,1,0:T(8,128)(2,1)}), bf16[64,16,1024]{2,1,0:T(8,128)(2,1)S(1)}, u32[]{:S(2)}, u32[]{:S(2)}) async-start(bf16[64,16,1024]{2,1,0:T(8,128)(2,1)} %bitcast.13), calls=%async_computation.2 | async-start | bytes 4194304 | tf_op jit(solution)/shard_map/all_to_all | solution.py:278

commit v4 on v3

--- a/solution.py
+++ b/solution.py
@@ -139,11 +139,15 @@
 
 
 def own_kernel(
-    x_ref, db_ref, dy_ref, gain_ref, router_ref, win_ref, wout_ref,
-    normed_ref, hid_ref, dpre_ref, part_ref, back_ref, small_ref,
+    x_ref, db_ref, dy_ref, pos_ref, gain_ref, router_ref, win_ref, wout_ref,
+    normed_ref, hid_ref, dpre_ref, base_ref, back_ref, small_ref, place_ref, gate_ref,
 ):
     slope, part = forward(x_ref, gain_ref, win_ref, wout_ref, normed_ref, hid_ref)
-    part_ref[...] = part
+    xf = x_ref[...].astype(F32)
+    gate = gate_of(xf, router_ref[...].astype(F32))
+    base_ref[...] = xf + gate * part
+    gate_ref[...] = jnp.broadcast_to(gate, gate_ref.shape)
+    place_ref[...] = mask(iota(place_ref.shape, 1).astype(F32) == pos_ref[:, :1])
     back, gain_part, router_part = backward(
         x_ref, db_ref, slope, part, gain_ref, router_ref, win_ref, wout_ref, dpre_ref
     )
@@ -186,17 +190,10 @@
     gout_ref[...] = dot(ho[...], bo[...], first) + dot(hp[...], bp[...], first)
 
 
-def spread(pos_ref, rows, out_ref):
-    place = mask(iota((out_ref.shape[0], rows.shape[0]), 1).astype(F32) == pos_ref[:, :1])
-    out_ref[...] = dot(place, rows, ((1,), (0,))).astype(BF)
-
-
-def mix_kernel(x_ref, part_ref, recv_ref, router_ref, pos_ref, out_ref, done_ref):
+def mix_kernel(base_ref, gate_ref, recv_ref, place_ref, out_ref, done_ref):
     done_ref[...] = jnp.zeros_like(done_ref)
-    xf = x_ref[...].astype(F32)
-    gate = gate_of(xf, router_ref[...].astype(F32))
-    rows = (xf + gate * (part_ref[...] + recv_ref[...].astype(F32))).astype(BF)
-    spread(pos_ref, rows, out_ref)
+    rows = (base_ref[...] + gate_ref[:, :1] * recv_ref[...].astype(F32)).astype(BF)
+    out_ref[...] = dot(place_ref[...], rows, ((1,), (0,))).astype(BF)
 
 
 def decode(ref, tok):
@@ -204,18 +201,17 @@
     return coded[0:2] + coded[2:4] + coded[4:6]
 
 
-def add_kernel(own_ref, tail_ref, recv_ref, pos_ref, out_ref, small_ref, recv, out, sems):
+def add_kernel(own_ref, tail_ref, recv_ref, place_ref, out_ref, small_ref, recv, out, sems):
     tok, slots = own_ref.shape[0], out.shape[0]
     loads = copies(pieces(recv_ref, recv, 3), sems)
     start(loads)
-    place = mask(iota((slots, tok), 1).astype(F32) == pos_ref[:, :1])
     wait(loads)
     rows = (own_ref[...] + recv[:tok, :].astype(F32)).astype(BF)
     step = slots // 2
     stores = []
     for part in range(2):
         at = pl.ds(part * step, step)
-        out[at, :] = dot(place[part * step : (part + 1) * step], rows, ((1,), (0,))).astype(BF)
+        out[at, :] = dot(place_ref[at, :], rows, ((1,), (0,))).astype(BF)
         group = copies(pieces(out.at[at], out_ref.at[at], 2), sems, 3 + 2 * part)
         start(group)
         stores += group
@@ -307,10 +303,11 @@
         compact_dy_kernel, "compact_dy", (rows_bf, rows_bf), place_cost, 4 * MIB, (buf, pos, x_own, router)
     )
     db_peer = swap(db_own)
-    normed_o, hid_o, dpre_o, part_o, back_o, small_o = call(
+    normed_o, hid_o, dpre_o, base_o, back_o, small_o, place, gate = call(
         own_kernel, "own",
-        (rows_bf, hid_bf, hid_bf, shape((tok, width), F32), shape((tok, width), F32), shape((2, width), F32)),
-        4 * mm, 14 * MIB, (x_own, db_own, dy_own, gain, router, win, wout),
+        (rows_bf, hid_bf, hid_bf, shape((tok, width), F32), shape((tok, width), F32), shape((2, width), F32),
+         shape((slots, tok), BF), shape((tok, 128), F32)),
+        4 * mm, 14 * MIB, (x_own, db_own, dy_own, pos, gain, router, win, wout),
     )
     normed_p, hid_p, slope_p, part_p = call(
         peer_forward_kernel, "peer_forward", (rows_bf, hid_bf, hid_bf, rows_bf),
@@ -323,7 +320,7 @@
     )
     back_recv = swap(back_p)
     y_pack, mix_done = call(
-        mix_kernel, "mix", (slots_bf, shape((8, 128), F32)), place_cost, 8 * MIB, (x_own, part_o, part_recv, router, pos)
+        mix_kernel, "mix", (slots_bf, shape((8, 128), F32)), place_cost, 8 * MIB, (base_o, gate, part_recv, place)
     )
     half = hidden // 2
     left = pl.BlockSpec((tok, half), lambda i: (0, i))
@@ -340,7 +337,7 @@
     y_buf = exchange(y_pack.reshape(experts, cap, width), experts).reshape(slots, width)
     back_pack, small = call(
         add_kernel, "add_back", (slots_bf, shape((2, width), F32)), place_cost, 5 * MIB,
-        (back_o, tail, back_recv, pos), grads_done, 24,
+        (back_o, tail, back_recv, place), grads_done, 24,
         in_specs=[inside, inside, outer, inside],
         out_specs=(outer, inside),
         scratch_shapes=[
@@ -351,11 +348,11 @@
     )
     back_pack, y_buf = lax.optimization_barrier((back_pack, y_buf))
     back_buf = exchange(back_pack.reshape(experts, cap, width), experts).reshape(slots, width)
-    mixed, place = call(
+    mixed, home = call(
         unpack_kernel, "unpack", (rows_bf, shape((tok, slots), BF)), place_cost, 4 * MIB, (slot, y_buf)
     )
     input_grad = call(
-        unpack_last_kernel, "unpack_last", rows_bf, place_cost, 4 * MIB, (place, back_buf), None, 40,
+        unpack_last_kernel, "unpack_last", rows_bf, place_cost, 4 * MIB, (home, back_buf), None, 40,
         in_specs=[inside, outer],
         out_specs=outer,
         scratch_shapes=[

time: 227 us -> 227 us (level)
  local copies, waits for them, and re-layouts: 11.5 us -> 19.1 us
  waiting for transfers between devices: 90 us -> 83.7 us
    unnamed x44 -> x50, local copies, waits for them, and re-layouts: 10.9 us -> 18.5 us
    ppermute x4, waiting for transfers between devices: 64.1 us -> 57.8 us  [swap(): return lax.ppermute(values, 'dp', SWAP)]
  transfers between devices with their start and end apart: 6 -> 6, of which waited for: 6 -> 6; matrix products, arithmetic and copies ran while one was open for 0% -> 0% of each run, Pallas kernels for 14% -> 13%
where the time goes in v4:
time: 227 us; the launch traced here: 226 us
  waiting for transfers between devices  83.7 us (37%)
  blocking collectives  62.1 us (27%)
  Pallas kernels  36.7 us (16%)
  starting transfers between devices  23.5 us (10%)
  local copies, waits for them, and re-layouts  19.1 us (8%)
    all_to_all x1, blocking collectives, exchange(): lax.all_to_all(buffer, 'expert', split_axis=0, concat_axis=0, tiled=True)  62.1 us
    ppermute x4, waiting for transfers between devices, swap(): return lax.ppermute(values, 'dp', SWAP)  57.8 us
    pallas_call x11, Pallas kernels, call(): pl.pallas_call(kernel, name=name, out_shape=out_shape, compiler_params=pl...  36.7 us
    all_to_all x2, waiting for transfers between devices, exchange(): lax.all_to_all(buffer, 'expert', split_axis=0, concat_axis=0, tiled=True)  25.9 us
    unnamed x50, local copies, waits for them, and re-layouts  18.5 us
    all_to_all x2, starting transfers between devices, exchange(): lax.all_to_all(buffer, 'expert', split_axis=0, concat_axis=0, tiled=True)  14.9 us
    ppermute x4, starting transfers between devices, swap(): return lax.ppermute(values, 'dp', SWAP)  8.55 us
  transfers between devices with their start and end apart: 6, of which 6 were waited for; matrix products, arithmetic and copies ran while one was open for 0% of the time, Pallas kernels for 13%

profile of v4, /device:TPU:1, one launch (start us, length us, event | category | flops | bytes accessed | tf_op | source)
XLA Modules:
  0.0 226.1 jit_solution(15143517509345969257)
XLA Ops:
  0.6 0.0 copy-start.8
  0.6 1.2 copy-done.8
  1.9 0.0 copy-start.9
  1.9 1.2 copy-done.9
  3.1 0.0 copy-start.14
  3.1 0.7 copy-done.14
  3.8 2.7 %pack.1 = (bf16[64,32,1024]{2,1,0:T(8,128)(2,1)S(1)}, s32[1,512]{1,0:T(1,128)S(1)}) custom-call(s32[1,512]{1,0:T(1,128)S(1)} %copy-done.14, bf16[512,1024]{1,0:T(8,128)(2,1)S(1)} %bitcast.21, bf16[512,1024]{1,0:T(8,128)(2,1)S(1)} %bitcast.22), custom_call_target="tpu_custom_call" | custom-call | flops 2147483648 | bytes 6291456 | tf_op jit(solution)/shard_map/pack/pallas_call | solution.py:255
  6.4 62.1 %all_to_all.15.buf_ref = bf16[64,32,1024]{2,1,0:T(8,128)(2,1)S(1)} all-to-all(bf16[64,32,1024]{2,1,0:T(8,128)(2,1)S(1)} %get-tuple-element.39), channel_id=1, replica_groups=mesh['expert'=64,'dp'=2] {'expert'}, dimensions={0} | all-to-all | bytes 8388608 | tf_op jit(solution)/shard_map/all_to_all | solution.py:274
  68.6 0.0 copy-start.6
  68.6 1.8 compact_x.1
  70.3 2.7 %collective-permute-start = (bf16[512,1024]{1,0:T(8,128)(2,1)S(1)}, bf16[512,1024]{1,0:T(8,128)(2,1)S(1)}, u32[]{:S(2)}, u32[]{:S(2)}) collective-permute-start(bf16[512,1024]{1,0:T(8,128)(2,1)S(1)} %get-tuple-element.40.x_ref), channel_id=1, source_target_pairs={{0,1},{1,0},{2,3},{3,2},{4,5},{5,4},{6,7},{7,6},{8,9},{9,8},{10,11... | collective-permute-start | bytes 3145736 | tf_op jit(solution)/shard_map/ppermute | solution.py:270
  73.0 0.0 copy-done.6
  73.0 0.0 copy-start.4
  73.0 0.0 copy-start.5
  73.0 0.0 copy-start.7
  73.0 1.4 compact_dy.1
  74.4 0.0 copy-start.10
  74.4 0.6 collective-permute-start.1
  75.0 0.0 copy-done.4
  75.0 0.2 copy-done.5
  75.3 0.0 copy-done.7
  75.3 6.3 %own.1 = (bf16[512,1024]{1,0:T(8,128)(2,1)S(1)}, bf16[512,1024]{1,0:T(8,128)(2,1)S(1)}, bf16[512,1024]{1,0:T(8,128)(2,1)S(1)}, f32[512,1024]{1,0:T(8,128)S(1)}, ...) custom-call(bf16[512,1024]{1,0:T(8,128)(2,1)S(1)} %get-tuple-element.40, ...), custom_call_target="tpu_custom_call" | custom-call | flops 4294967296 | bytes 14680064 | tf_op jit(solution)/shard_map/own/pallas_call | solution.py:255
  81.6 0.0 copy-done.10
  81.6 0.0 copy-start.19
  81.6 1.0 copy-done.19
  82.6 0.0 copy-start.21
  82.6 13.9 %collective-permute-done.refs_0_.x_ref = bf16[512,1024]{1,0:T(8,128)(2,1)S(1)} collective-permute-done((bf16[512,1024]{1,0:T(8,128)(2,1)S(1)}, bf16[512,1024]{1,0:T(8,128)(2,1)S(1)}, u32[]{:S(2)}, u32[]{:S(2)}) %collective-permute-start) | collective-permute-done | bytes 1048608 | tf_op jit(solution)/shard_map/ppermute | solution.py:270
  96.5 2.8 %peer_forward.1 = (bf16[512,1024]{1,0:T(8,128)(2,1)S(1)}, bf16[512,1024]{1,0:T(8,128)(2,1)S(1)}, bf16[512,1024]{1,0:T(8,128)(2,1)S(1)}, bf16[512,1024]{1,0:T(8,128)(2,1)S(1)}) custom-call(bf16[512,1024]{1,0:T(8,128)(2,1)S(1)} %collective-permute-done.refs_0_.x_ref, f32[1,1024]{1,0:T(1,128)S(1)} %copy-done.7, bf16[1024,1024]{1,0:T(8,128)(2,1)S(1)} %bitcast.16, ...), custom_call_target="tpu_custom_call" | custom-call | flops 2147483648 | bytes 9437184 | tf_op jit(solution)/shard_map/peer_forward/pallas_call | solution.py:255
  99.3 0.0 copy-done.21
  99.3 0.0 copy-done.23
  99.3 0.0 copy-start.15
  99.3 1.0 copy-done.15
  100.3 1.0 copy-done.17
  101.3 2.6 %collective-permute-start.3 = (bf16[512,1024]{1,0:T(8,128)(2,1)S(1)}, bf16[512,1024]{1,0:T(8,128)(2,1)S(1)}, u32[]{:S(2)}, u32[]{:S(2)}) collective-permute-start(bf16[512,1024]{1,0:T(8,128)(2,1)S(1)} %get-tuple-element.47.part_ref), channel_id=1, source_target_pairs={{0,1},{1,0},{2,3},{3,2},{4,5},{5,4},{6,7},{7,6},{8,9},{9,8},{10,11... | collective-permute-start | bytes 3145736 | tf_op jit(solution)/shard_map/ppermute | solution.py:270
  103.9 15.1 %collective-permute-done.1.db_ref.refs_7_ = bf16[512,1024]{1,0:T(8,128)(2,1)S(1)} collective-permute-done((bf16[512,1024]{1,0:T(8,128)(2,1)S(1)}, bf16[512,1024]{1,0:T(8,128)(2,1)S(1)}, u32[]{:S(2)}, u32[]{:S(2)}) %collective-permute-start.1) | collective-permute-done | bytes 1048608 | tf_op jit(solution)/shard_map/ppermute | solution.py:270
  119.0 4.6 %peer_backward.1 = (bf16[512,1024]{1,0:T(8,128)(2,1)S(1)}, bf16[528,1024]{1,0:T(8,128)(2,1)}, bf16[16,1024]{1,0:T(8,128)(2,1)S(1)}) custom-call(bf16[512,1024]{1,0:T(8,128)(2,1)S(1)} %collective-permute-done.refs_0_.x_ref, bf16[512,1024]{1,0:T(8,128)(2,1)S(1)} %collective-permute-done.1.db_ref.refs_7_, bf16[512,1024]{1,0:T(8,128)(2,1)S(1)} %get-tuple-element.46.slope_ref, ...), custom_call_target="tpu_custom_call" | custom-call | flops 2147483648 | bytes 9437184 | tf_op jit(solution)/shard_map/peer_backward/pallas_call | solution.py:255
  123.6 1.0 copy-done.12
  124.5 2.6 %collective-permute-start.2 = (bf16[528,1024]{1,0:T(8,128)(2,1)}, bf16[528,1024]{1,0:T(8,128)(2,1)}, u32[]{:S(2)}, u32[]{:S(2)}) collective-permute-start(bf16[528,1024]{1,0:T(8,128)(2,1)} %get-tuple-element.49), channel_id=1, source_target_pairs={{0,1},{1,0},{2,3},{3,2},{4,5},{5,4},{6,7},{7,6},{8,9},{9,8},{10,11... | collective-permute-start | bytes 3244040 | tf_op jit(solution)/shard_map/ppermute | solution.py:270
  127.2 14.3 %collective-permute-done.3.recv_ref = bf16[512,1024]{1,0:T(8,128)(2,1)S(1)} collective-permute-done((bf16[512,1024]{1,0:T(8,128)(2,1)S(1)}, bf16[512,1024]{1,0:T(8,128)(2,1)S(1)}, u32[]{:S(2)}, u32[]{:S(2)}) %collective-permute-start.3) | collective-permute-done | bytes 1048608 | tf_op jit(solution)/shard_map/ppermute | solution.py:270
  141.4 0.0 copy-done
  141.4 1.4 mix.1
  142.8 0.0 copy-start.2
  142.8 1.3 copy-done.2
  144.1 7.8 %all-to-all-start.1 = ((bf16[64,16,1024]{2,1,0:T(8,128)(2,1)}), bf16[64,16,1024]{2,1,0:T(8,128)(2,1)}, u32[]{:S(2)}, u32[]{:S(2)}) async-start(bf16[64,16,1024]{2,1,0:T(8,128)(2,1)} %bitcast.13), calls=%async_computation.1 | async-start | bytes 4194304 | tf_op jit(solution)/shard_map/all_to_all | solution.py:274
  151.9 0.0 copy-start.11
  151.9 1.2 copy-done.11
  153.1 1.2 copy-done.13
  154.4 1.2 copy-done.16
  155.6 1.2 copy-done.18
  156.8 1.2 copy-done.20
  158.0 1.2 copy-done.22
  159.3 1.2 copy-done.24
  160.5 6.5 %weight_grads.1 = (f32[1024,1024]{1,0:T(8,128)}, f32[1024,1024]{1,0:T(8,128)}, f32[8,128]{1,0:T(8,128)S(1)}) custom-call(bf16[512,1024]{1,0:T(8,128)(2,1)S(1)} %copy-done.24, bf16[512,1024]{1,0:T(8,128)(2,1)S(1)} %copy-done.13, bf16[512,1024]{1,0:T(8,128)(2,1)S(1)} %copy-done.20, bf16[512,1024]{1,0:T(8,128)(2,1)S(1)} %copy-done.16, ...), custom_call_target="tpu_custom_call" | custom-call | flops 999999995904 | bytes 16777216 | tf_op jit(solution)/shard_map/weight_grads/pallas_call | solution.py:255
  167.0 14.6 %collective-permute-done.2.refs_2_ = bf16[528,1024]{1,0:T(8,128)(2,1)} collective-permute-done((bf16[528,1024]{1,0:T(8,128)(2,1)}, bf16[528,1024]{1,0:T(8,128)(2,1)}, u32[]{:S(2)}, u32[]{:S(2)}) %collective-permute-start.2) | collective-permute-done | bytes 1081376 | tf_op jit(solution)/shard_map/ppermute | solution.py:270
  181.6 0.0 copy-done.1
  181.6 2.9 %add_back.1 = (bf16[1024,1024]{1,0:T(8,128)(2,1)S(1)}, f32[2,1024]{1,0:T(2,128)S(1)}) custom-call(f32[512,1024]{1,0:T(8,128)S(1)} %get-tuple-element.44.refs_0_, bf16[16,1024]{1,0:T(8,128)(2,1)S(1)} %get-tuple-element.48.refs_1_, bf16[528,1024]{1,0:T(8,128)(2,1)} %collective-permute-done.2.refs_2_, bf16[1024,512]{1,0:T(8,128)(2,1)S(1)} %copy-done.1, ...), custom_call_target="tpu_custom_call" | custom-call | flops 1073741824 | bytes 5242880 | tf_op jit(solution)/shard_map/add_back/pallas_call | solution.py:255
  184.4 0.0 copy-start.3
  184.4 1.4 copy-done.3
  185.8 1.7 all-to-all-done.1
  187.5 7.2 %all-to-all-start.2 = ((bf16[64,16,1024]{2,1,0:T(8,128)(2,1)}), bf16[64,16,1024]{2,1,0:T(8,128)(2,1)S(1)}, u32[]{:S(2)}, u32[]{:S(2)}) async-start(bf16[64,16,1024]{2,1,0:T(8,128)(2,1)} %bitcast.14), calls=%async_computation.2 | async-start | bytes 4194304 | tf_op jit(solution)/shard_map/all_to_all | solution.py:274
  194.7 0.6 fusion
  195.3 4.2 %unpack.1 = (bf16[512,1024]{1,0:T(8,128)(2,1)}, bf16[512,1024]{1,0:T(8,128)(2,1)S(1)}) custom-call(s32[1,512]{1,0:T(1,128)S(1)} %get-tuple-element.38.slot_ref, bf16[1024,1024]{1,0:T(8,128)(2,1)} %bitcast.5.buf_ref), custom_call_target="tpu_custom_call" | custom-call | flops 1073741824 | bytes 4194304 | tf_op jit(solution)/shard_map/unpack/pallas_call | solution.py:255
  199.4 24.2 %all-to-all-done.2 = bf16[64,16,1024]{2,1,0:T(8,128)(2,1)S(1)} async-done(((bf16[64,16,1024]{2,1,0:T(8,128)(2,1)}), bf16[64,16,1024]{2,1,0:T(8,128)(2,1)S(1)}, u32[]{:S(2)}, u32[]{:S(2)}) %all-to-all-start.2) | async-done | bytes 2097184 | tf_op jit(solution)/shard_map/all_to_all | solution.py:274
  223.7 2.3 unpack_last.1
  (11 shorter events, 0.0 us)
Async XLA Ops:
  0.6 1.2 copy-start.8
  1.9 1.2 copy-start.9
  3.1 0.7 copy-start.14
  68.6 4.5 %copy-start.6 = (bf16[1,1024]{1,0:T(2,128)(2,1)S(1)}, bf16[1,1024]{1,0:T(2,128)(2,1)}, u32[]{:S(2)}) copy-start(bf16[1,1024]{1,0:T(2,128)(2,1)} %router_ref.5) | copy-start | bytes 6148
  70.3 26.2 %collective-permute-start = (bf16[512,1024]{1,0:T(8,128)(2,1)S(1)}, bf16[512,1024]{1,0:T(8,128)(2,1)S(1)}, u32[]{:S(2)}, u32[]{:S(2)}) collective-permute-start(bf16[512,1024]{1,0:T(8,128)(2,1)S(1)} %get-tuple-element.40.x_ref), channel_id=1, source_target_pairs={{0,1},{1,0},{2,3},{3,2},{4,5},{5,4},{6,7},{7,6},{8,9},{9,8},{10,11... | collective-permute-start | bytes 3145736 | tf_op jit(solution)/shard_map/ppermute | solution.py:270
  73.0 2.0 copy-start.4
  73.0 2.2 copy-start.5
  73.0 2.2 copy-start.7
  74.4 7.2 %copy-start.10 = (bf16[512,1024]{1,0:T(8,128)(2,1)}, bf16[512,1024]{1,0:T(8,128)(2,1)S(1)}, u32[]{:S(2)}) copy-start(bf16[512,1024]{1,0:T(8,128)(2,1)S(1)} %get-tuple-element.42.db_ref.refs_6_) | copy-start | bytes 3145732
  74.4 44.5 %collective-permute-start.1 = (bf16[512,1024]{1,0:T(8,128)(2,1)S(1)}, bf16[512,1024]{1,0:T(8,128)(2,1)S(1)}, u32[]{:S(2)}, u32[]{:S(2)}) collective-permute-start(bf16[512,1024]{1,0:T(8,128)(2,1)S(1)} %get-tuple-element.42.db_ref.refs_6_), channel_id=1, source_target_pairs={{0,1},{1,0},{2,3},{3,2},{4,5},{5,4},{6,7},{7,6},{8,9},{9,8},{10,11... | collective-permute-start | bytes 3145736 | tf_op jit(solution)/shard_map/ppermute | solution.py:270
  81.6 1.0 copy-start.19
  82.6 16.7 %copy-start.21 = (bf16[512,1024]{1,0:T(8,128)(2,1)}, bf16[512,1024]{1,0:T(8,128)(2,1)S(1)}, u32[]{:S(2)}) copy-start(bf16[512,1024]{1,0:T(8,128)(2,1)S(1)} %get-tuple-element.55.refs_4_) | copy-start | bytes 3145732
  82.6 16.8 %copy-start.23 = (bf16[512,1024]{1,0:T(8,128)(2,1)}, bf16[512,1024]{1,0:T(8,128)(2,1)S(1)}, u32[]{:S(2)}) copy-start(bf16[512,1024]{1,0:T(8,128)(2,1)S(1)} %get-tuple-element.51.refs_0_) | copy-start | bytes 3145732
  82.6 58.9 %copy-start = (bf16[1024,512]{1,0:T(8,128)(2,1)}, bf16[1024,512]{1,0:T(8,128)(2,1)S(1)}, u32[]{:S(2)}) copy-start(bf16[1024,512]{1,0:T(8,128)(2,1)S(1)} %get-tuple-element.50.place_ref.refs_3_) | copy-start | bytes 3145732
  99.3 1.0 copy-start.15
  100.3 1.0 copy-start.17
  101.3 40.2 %collective-permute-start.3 = (bf16[512,1024]{1,0:T(8,128)(2,1)S(1)}, bf16[512,1024]{1,0:T(8,128)(2,1)S(1)}, u32[]{:S(2)}, u32[]{:S(2)}) collective-permute-start(bf16[512,1024]{1,0:T(8,128)(2,1)S(1)} %get-tuple-element.47.part_ref), channel_id=1, source_target_pairs={{0,1},{1,0},{2,3},{3,2},{4,5},{5,4},{6,7},{7,6},{8,9},{9,8},{10,11... | collective-permute-start | bytes 3145736 | tf_op jit(solution)/shard_map/ppermute | solution.py:270
  123.6 1.0 copy-start.12
  124.5 57.0 %collective-permute-start.2 = (bf16[528,1024]{1,0:T(8,128)(2,1)}, bf16[528,1024]{1,0:T(8,128)(2,1)}, u32[]{:S(2)}, u32[]{:S(2)}) collective-permute-start(bf16[528,1024]{1,0:T(8,128)(2,1)} %get-tuple-element.49), channel_id=1, source_target_pairs={{0,1},{1,0},{2,3},{3,2},{4,5},{5,4},{6,7},{7,6},{8,9},{9,8},{10,11... | collective-permute-start | bytes 3244040 | tf_op jit(solution)/shard_map/ppermute | solution.py:270
  142.8 1.3 copy-start.2
  144.1 43.3 %all-to-all-start.1 = ((bf16[64,16,1024]{2,1,0:T(8,128)(2,1)}), bf16[64,16,1024]{2,1,0:T(8,128)(2,1)}, u32[]{:S(2)}, u32[]{:S(2)}) async-start(bf16[64,16,1024]{2,1,0:T(8,128)(2,1)} %bitcast.13), calls=%async_computation.1 | async-start | bytes 4194304 | tf_op jit(solution)/shard_map/all_to_all | solution.py:274
  151.9 1.2 copy-start.11
  153.1 1.2 copy-start.13
  154.4 1.2 copy-start.16
  155.6 1.2 copy-start.18
  156.8 1.2 copy-start.20
  158.0 1.2 copy-start.22
  159.3 1.2 copy-start.24
  160.5 21.1 %copy-start.1 = (bf16[1024,512]{1,0:T(8,128)(2,1)S(1)}, bf16[1024,512]{1,0:T(8,128)(2,1)}, u32[]{:S(2)}) copy-start(bf16[1024,512]{1,0:T(8,128)(2,1)} %copy-done) | copy-start | bytes 3145732
  184.4 1.4 copy-start.3
  187.5 36.2 %all-to-all-start.2 = ((bf16[64,16,1024]{2,1,0:T(8,128)(2,1)}), bf16[64,16,1024]{2,1,0:T(8,128)(2,1)S(1)}, u32[]{:S(2)}, u32[]{:S(2)}) async-start(bf16[64,16,1024]{2,1,0:T(8,128)(2,1)} %bitcast.14), calls=%async_computation.2 | async-start | bytes 4194304 | tf_op jit(solution)/shard_map/all_to_all | solution.py:274
